TPU v7x, 128 devices: a whole 4x4x4 slice. The times are simulated.
128 devices in a mesh: row: 8 (over x, core), col: 16 (over z, y).
Axes of the slice: x: 4, y: 4, z: 4, core: 2. Of those that a mesh axis runs over, the one named last changes fastest.
Arguments:
- leaf_up: bfloat16 [65536, 3, 128], P(('row', 'col')), may hold values from -6 to 6
- child_to_parent: bfloat16 [8, 128, 128], replicated, may hold values from -0.1875 to 0.1875
- translations: bfloat16 [316, 128, 128], replicated, may hold values from -0.0390625 to 0.0390625
- parent_to_child: bfloat16 [8, 128, 128], replicated, may hold values from -0.5 to 0.5
- check_to_density: bfloat16 [128, 128], replicated, may hold values from -0.375 to 0.375
- leaf_lists: int32 [65536, 316], P(('row', 'col')), may hold values from -1 to 4607
- leaf_ghosts: int32 [128, 16, 256], P(('row', 'col')), may hold values from 0 to 511, as said below
- parent_lists: int32 [8192, 316], P(('row', 'col')), may hold values from -1 to 575, as said below
- parent_ghosts: int32 [128, 16, 32], P(('row', 'col')), may hold values from 0 to 63, as said below
Outputs:
- leaf_down: bfloat16 [65536, 3, 128], P(('row', 'col'))
Inputs may be any that keep to these rules, and one draw needn't show every extreme that they name: The 256 entries of leaf_ghosts[e, j, :] are distinct. `parent_lists`: sources of a parent lie in its own row of devices. The 32 entries of parent_ghosts[e, c, :] are distinct.
All inputs are finite; a program needn't handle non-finite values.
Results may differ from a plain program's by a relative error of at most 0.0075.
Values may be sent and summed in bfloat16 or wider, within the bound.
No kernel may reach another device: no remote copies, remote signals or barrier semaphores. Data moves between devices by JAX's collectives and lax.ppermute only.
A program may use at most 128 MiB of HBM per device.

v0:
```python
import jax
import jax.numpy as jnp
from jax import lax
from jax.sharding import PartitionSpec as P


def from_behind(value, axis, steps):
    count = lax.axis_size(axis)
    first, last = (max(0, -steps), min(count, count - steps))
    return lax.ppermute(value, axis, [(source, source + steps) for source in range(first, last)])


def translate(sources, position, table):
    box_count = position.shape[0]
    block = min(box_count, 256)
    points = table.shape[-1]
    groups = 4
    per_group = table.shape[0] // groups
    padded = jnp.concatenate([sources, jnp.zeros((1, 3, points), sources.dtype)], axis=0)
    planes = padded.transpose(1, 0, 2)
    chosen = jnp.where(position < 0, sources.shape[0], position)
    chosen = chosen.reshape(box_count // block, block, groups, per_group).transpose(0, 2, 3, 1)
    grouped_table = table.reshape(groups, per_group, points, points)

    def per_block(indices):

        def step(total, item):
            picked, operators = item
            gathered = jnp.take(planes, picked.reshape(-1), axis=1).reshape(
                3, per_group, block, points
            )
            return (
                total
                + jnp.einsum(
                    "ktbp,tqp->kbq", gathered, operators, preferred_element_type=jnp.float32
                ),
                None,
            )

        total, _ = lax.scan(
            step, jnp.zeros((3, block, points), jnp.float32), (indices, grouped_table)
        )
        return total

    result = lax.map(per_block, chosen)
    return result.transpose(0, 2, 1, 3).reshape(box_count, 3, points)


def rank_distance(which, near_count):
    if which < near_count:
        return which + 1
    return -(which - near_count + 1)


def local(
    leaf_up,
    child_to_parent,
    translations,
    parent_to_child,
    check_to_density,
    leaf_lists,
    leaf_ghosts,
    parent_lists,
    parent_ghosts,
):
    points = leaf_up.shape[-1]
    leaf_count = leaf_up.shape[0]
    parents = leaf_count // 8
    grouped = leaf_up.reshape(parents, 8, 3, points)
    parent_up = jnp.einsum(
        "bckp,cqp->bkq", grouped, child_to_parent, preferred_element_type=jnp.float32
    ).astype(jnp.bfloat16)
    outgoing = leaf_up[leaf_ghosts[0]]
    offsets = outgoing.shape[0]
    near_count = offsets // 2
    received = []
    for which in range(offsets):
        received.append(
            from_behind(outgoing[which], ("row", "col"), rank_distance(which, near_count))
        )
    arrived = jnp.stack(received, axis=0)
    leaf_sources = jnp.concatenate([leaf_up, arrived.reshape(-1, 3, points)], axis=0)
    parent_sent = parent_up[parent_ghosts[0]]
    parent_came = lax.all_to_all(parent_sent, "col", split_axis=0, concat_axis=0, tiled=True)
    parent_sources = jnp.concatenate([parent_up, parent_came.reshape(-1, 3, points)], axis=0)
    parent_check = translate(parent_sources, parent_lists, translations).astype(jnp.bfloat16)
    parent_down = jnp.einsum(
        "bkp,qp->bkq", parent_check, check_to_density, preferred_element_type=jnp.float32
    ).astype(jnp.bfloat16)
    from_parent = jnp.einsum(
        "bkp,cqp->bckq", parent_down, parent_to_child, preferred_element_type=jnp.float32
    ).reshape(leaf_count, 3, points)
    leaf_check = (from_parent + translate(leaf_sources, leaf_lists, translations)).astype(
        jnp.bfloat16
    )
    return jnp.einsum(
        "bkp,qp->bkq", leaf_check, check_to_density, preferred_element_type=jnp.float32
    ).astype(jnp.bfloat16)


def solution(mesh):
    return jax.shard_map(
        local,
        mesh=mesh,
        in_specs=(
            P(("row", "col"), None, None),
            P(),
            P(),
            P(),
            P(),
            P(("row", "col"), None),
            P(("row", "col"), None, None),
            P(("row", "col"), None),
            P(("row", "col"), None, None),
        ),
        out_specs=P(("row", "col"), None, None),
        check_vma=False,
    )
```

profile of v0, /device:TPU:3, one launch (start us, length us, event | category | flops | bytes accessed | tf_op | source)
XLA Modules:
  0.0 855.8 jit_solution(4348358586041935821)
XLA Ops:
  0.8 37.7 %gather_fusion.3 = bf16[4096,3,128]{2,0,1:T(8,128)(2,1)} fusion(bf16[512,3,128]{2,0,1:T(8,128)(2,1)} %param.15, s32[4096]{0:T(1024)S(1)} %broadcast_clamp_fusion), kind=kCustom, calls=%fused_computation.3 | custom fusion | bytes 6307840 | tf_op jit(solution)/shard_map/gather | solution.py:73
  38.5 3.6 fusion.41
  42.1 3.2 collective-permute-start
  45.3 4.5 collective-permute-start.1
  49.9 4.3 collective-permute-start.2
  54.2 3.5 collective-permute-start.3
  57.8 3.4 collective-permute-start.4
  65.0 8.4 all-to-all-start
  76.8 5.6 collective-permute-start.5
  83.3 4.3 collective-permute-start.6
  88.6 2.8 collective-permute-start.7
  92.4 3.7 collective-permute-start.8
  97.1 3.7 collective-permute-start.9
  101.7 3.6 collective-permute-start.10
  105.4 3.0 collective-permute-start.11
  108.5 5.2 collective-permute-start.12
  113.7 3.7 collective-permute-start.13
  119.8 3.9 collective-permute-start.15
  123.9 4.9 collective-permute-done.14
  131.7 19.3 %copy.59 = bf16[3,4609,128]{2,0,1:T(4,128)(2,1)} copy(bf16[3,4609,128]{2,1,0:T(8,128)(2,1)S(1)} %maximum_bitcast_fusion) | data formatting | bytes 7079424 | tf_op jit(solution)/shard_map/while | solution.py:45
  151.0 535.1 %while.40 = (s32[]{:T(128)}, f32[2,3,256,128]{3,2,0,1:T(8,128)S(1)}, s32[2,4,79,256]{3,0,2,1:T(2,128)S(1)}, bf16[3,4609,128]{2,0,1:T(4,128)(2,1)}, bf16[4,79,128...) while((s32[]{:T(128)}, f32[2,3,256,128]{3,2,0,1:T(8,128)S(1)}, ...), condition=%wide.region_5.6_spmd, body=%wide.region_2.5_spmd.sunk | while | flops 1996265216 | bytes 58080512 | solution.py:45
  151.3 267.2 %while.42 = (s32[]{:T(128)}, f32[3,256,128]{2,1,0:T(8,128)S(1)}, s32[4,79,256]{2,1,0:T(8,128)S(1)}, bf16[3,4609,128]{2,0,1:T(4,128)(2,1)}, bf16[4,79,128,128]{3,2,1,0:T(8,128)(2,1)}, /*index=5*/s32[]{:T(128)}, s32[]{:T(128)}) while((s32[]{:T(128)}, f32[3,256,128]{2,1,0:T(8,128)S(1)}, s32[4,79,256]{2,1,0:T(8,128)S(1)}, ...), condition=%wide.region_4.4_spmd.clone, body=%wide.region_3.3_spmd.clone.sunk | while | flops 1996265216 | bytes 55999580 | solution.py:40
  151.7 55.0 %gather_fusion.1 = bf16[20224,3,128]{2,1,0:T(4,128)(2,1)} fusion(bf16[3,4609,128]{2,0,1:T(4,128)(2,1)} %get-tuple-element.348, s32[20480]{0:T(1024)S(1)} %pad_clamp_fusion.6), kind=kCustom, calls=%fused_computation.1.clone.clone.1 | custom fusion | bytes 31144960 | tf_op jit(solution)/shard_map/while/body/eval_jaxpr/while/body/eval_jaxpr/jit(_take)/gather | solution.py:29
  206.8 11.4 %fusion.52 = f32[3,256,128]{2,1,0:T(8,128)S(1)} fusion(bf16[4,79,128,128]{3,2,1,0:T(8,128)(2,1)} %get-tuple-element.349, s32[]{:T(128)} %get-tuple-element.338, bf16[3,79,256,128]{3,0,2,1:T(4,128)(2,1)} %bitcast.177, pred[79,256]{1,0:T(8,128)(4,1)S(1)} %compare_and_fusion.5, f32[3,256,128]{2,1,0:T(8,128)S(1)} %get-tuple-element.339, pred[]{:T(512)S(6)} %compare.7), kind=kOutput, calls=%fused_computation.26.clone.1 | convolution fusion | flops 1996062720 | bytes 24105216 | tf_op jit(solution)/shard_map/while/body/eval_jaxpr/while/body/eval_jaxpr/ktbp,tqp->kbq/dot_general | solution.py:34
  218.5 55.0 %gather_fusion.1 = bf16[20224,3,128]{2,1,0:T(4,128)(2,1)} fusion(bf16[3,4609,128]{2,0,1:T(4,128)(2,1)} %get-tuple-element.348, s32[20480]{0:T(1024)S(1)} %pad_clamp_fusion.6), kind=kCustom, calls=%fused_computation.1.clone.clone.1 | custom fusion | bytes 31144960 | tf_op jit(solution)/shard_map/while/body/eval_jaxpr/while/body/eval_jaxpr/jit(_take)/gather | solution.py:29
  273.5 11.4 %fusion.52 = f32[3,256,128]{2,1,0:T(8,128)S(1)} fusion(bf16[4,79,128,128]{3,2,1,0:T(8,128)(2,1)} %get-tuple-element.349, s32[]{:T(128)} %get-tuple-element.338, bf16[3,79,256,128]{3,0,2,1:T(4,128)(2,1)} %bitcast.177, pred[79,256]{1,0:T(8,128)(4,1)S(1)} %compare_and_fusion.5, f32[3,256,128]{2,1,0:T(8,128)S(1)} %get-tuple-element.339, pred[]{:T(512)S(6)} %compare.7), kind=kOutput, calls=%fused_computation.26.clone.1 | convolution fusion | flops 1996062720 | bytes 24105216 | tf_op jit(solution)/shard_map/while/body/eval_jaxpr/while/body/eval_jaxpr/ktbp,tqp->kbq/dot_general | solution.py:34
  285.3 55.0 %gather_fusion.1 = bf16[20224,3,128]{2,1,0:T(4,128)(2,1)} fusion(bf16[3,4609,128]{2,0,1:T(4,128)(2,1)} %get-tuple-element.348, s32[20480]{0:T(1024)S(1)} %pad_clamp_fusion.6), kind=kCustom, calls=%fused_computation.1.clone.clone.1 | custom fusion | bytes 31144960 | tf_op jit(solution)/shard_map/while/body/eval_jaxpr/while/body/eval_jaxpr/jit(_take)/gather | solution.py:29
  340.3 11.4 %fusion.52 = f32[3,256,128]{2,1,0:T(8,128)S(1)} fusion(bf16[4,79,128,128]{3,2,1,0:T(8,128)(2,1)} %get-tuple-element.349, s32[]{:T(128)} %get-tuple-element.338, bf16[3,79,256,128]{3,0,2,1:T(4,128)(2,1)} %bitcast.177, pred[79,256]{1,0:T(8,128)(4,1)S(1)} %compare_and_fusion.5, f32[3,256,128]{2,1,0:T(8,128)S(1)} %get-tuple-element.339, pred[]{:T(512)S(6)} %compare.7), kind=kOutput, calls=%fused_computation.26.clone.1 | convolution fusion | flops 1996062720 | bytes 24105216 | tf_op jit(solution)/shard_map/while/body/eval_jaxpr/while/body/eval_jaxpr/ktbp,tqp->kbq/dot_general | solution.py:34
  352.1 55.0 %gather_fusion.1 = bf16[20224,3,128]{2,1,0:T(4,128)(2,1)} fusion(bf16[3,4609,128]{2,0,1:T(4,128)(2,1)} %get-tuple-element.348, s32[20480]{0:T(1024)S(1)} %pad_clamp_fusion.6), kind=kCustom, calls=%fused_computation.1.clone.clone.1 | custom fusion | bytes 31144960 | tf_op jit(solution)/shard_map/while/body/eval_jaxpr/while/body/eval_jaxpr/jit(_take)/gather | solution.py:29
  407.1 11.4 %fusion.52 = f32[3,256,128]{2,1,0:T(8,128)S(1)} fusion(bf16[4,79,128,128]{3,2,1,0:T(8,128)(2,1)} %get-tuple-element.349, s32[]{:T(128)} %get-tuple-element.338, bf16[3,79,256,128]{3,0,2,1:T(4,128)(2,1)} %bitcast.177, pred[79,256]{1,0:T(8,128)(4,1)S(1)} %compare_and_fusion.5, f32[3,256,128]{2,1,0:T(8,128)S(1)} %get-tuple-element.339, pred[]{:T(512)S(6)} %compare.7), kind=kOutput, calls=%fused_computation.26.clone.1 | convolution fusion | flops 1996062720 | bytes 24105216 | tf_op jit(solution)/shard_map/while/body/eval_jaxpr/while/body/eval_jaxpr/ktbp,tqp->kbq/dot_general | solution.py:34
  418.9 267.2 %while.42 = (s32[]{:T(128)}, f32[3,256,128]{2,1,0:T(8,128)S(1)}, s32[4,79,256]{2,1,0:T(8,128)S(1)}, bf16[3,4609,128]{2,0,1:T(4,128)(2,1)}, bf16[4,79,128,128]{3,2,1,0:T(8,128)(2,1)}, /*index=5*/s32[]{:T(128)}, s32[]{:T(128)}) while((s32[]{:T(128)}, f32[3,256,128]{2,1,0:T(8,128)S(1)}, s32[4,79,256]{2,1,0:T(8,128)S(1)}, ...), condition=%wide.region_4.4_spmd.clone, body=%wide.region_3.3_spmd.clone.sunk | while | flops 1996265216 | bytes 55999580 | solution.py:40
  419.3 55.0 %gather_fusion.1 = bf16[20224,3,128]{2,1,0:T(4,128)(2,1)} fusion(bf16[3,4609,128]{2,0,1:T(4,128)(2,1)} %get-tuple-element.348, s32[20480]{0:T(1024)S(1)} %pad_clamp_fusion.6), kind=kCustom, calls=%fused_computation.1.clone.clone.1 | custom fusion | bytes 31144960 | tf_op jit(solution)/shard_map/while/body/eval_jaxpr/while/body/eval_jaxpr/jit(_take)/gather | solution.py:29
  474.3 11.4 %fusion.52 = f32[3,256,128]{2,1,0:T(8,128)S(1)} fusion(bf16[4,79,128,128]{3,2,1,0:T(8,128)(2,1)} %get-tuple-element.349, s32[]{:T(128)} %get-tuple-element.338, bf16[3,79,256,128]{3,0,2,1:T(4,128)(2,1)} %bitcast.177, pred[79,256]{1,0:T(8,128)(4,1)S(1)} %compare_and_fusion.5, f32[3,256,128]{2,1,0:T(8,128)S(1)} %get-tuple-element.339, pred[]{:T(512)S(6)} %compare.7), kind=kOutput, calls=%fused_computation.26.clone.1 | convolution fusion | flops 1996062720 | bytes 24105216 | tf_op jit(solution)/shard_map/while/body/eval_jaxpr/while/body/eval_jaxpr/ktbp,tqp->kbq/dot_general | solution.py:34
  486.1 55.0 %gather_fusion.1 = bf16[20224,3,128]{2,1,0:T(4,128)(2,1)} fusion(bf16[3,4609,128]{2,0,1:T(4,128)(2,1)} %get-tuple-element.348, s32[20480]{0:T(1024)S(1)} %pad_clamp_fusion.6), kind=kCustom, calls=%fused_computation.1.clone.clone.1 | custom fusion | bytes 31144960 | tf_op jit(solution)/shard_map/while/body/eval_jaxpr/while/body/eval_jaxpr/jit(_take)/gather | solution.py:29
  541.1 11.4 %fusion.52 = f32[3,256,128]{2,1,0:T(8,128)S(1)} fusion(bf16[4,79,128,128]{3,2,1,0:T(8,128)(2,1)} %get-tuple-element.349, s32[]{:T(128)} %get-tuple-element.338, bf16[3,79,256,128]{3,0,2,1:T(4,128)(2,1)} %bitcast.177, pred[79,256]{1,0:T(8,128)(4,1)S(1)} %compare_and_fusion.5, f32[3,256,128]{2,1,0:T(8,128)S(1)} %get-tuple-element.339, pred[]{:T(512)S(6)} %compare.7), kind=kOutput, calls=%fused_computation.26.clone.1 | convolution fusion | flops 1996062720 | bytes 24105216 | tf_op jit(solution)/shard_map/while/body/eval_jaxpr/while/body/eval_jaxpr/ktbp,tqp->kbq/dot_general | solution.py:34
  552.9 55.0 %gather_fusion.1 = bf16[20224,3,128]{2,1,0:T(4,128)(2,1)} fusion(bf16[3,4609,128]{2,0,1:T(4,128)(2,1)} %get-tuple-element.348, s32[20480]{0:T(1024)S(1)} %pad_clamp_fusion.6), kind=kCustom, calls=%fused_computation.1.clone.clone.1 | custom fusion | bytes 31144960 | tf_op jit(solution)/shard_map/while/body/eval_jaxpr/while/body/eval_jaxpr/jit(_take)/gather | solution.py:29
  607.9 11.4 %fusion.52 = f32[3,256,128]{2,1,0:T(8,128)S(1)} fusion(bf16[4,79,128,128]{3,2,1,0:T(8,128)(2,1)} %get-tuple-element.349, s32[]{:T(128)} %get-tuple-element.338, bf16[3,79,256,128]{3,0,2,1:T(4,128)(2,1)} %bitcast.177, pred[79,256]{1,0:T(8,128)(4,1)S(1)} %compare_and_fusion.5, f32[3,256,128]{2,1,0:T(8,128)S(1)} %get-tuple-element.339, pred[]{:T(512)S(6)} %compare.7), kind=kOutput, calls=%fused_computation.26.clone.1 | convolution fusion | flops 1996062720 | bytes 24105216 | tf_op jit(solution)/shard_map/while/body/eval_jaxpr/while/body/eval_jaxpr/ktbp,tqp->kbq/dot_general | solution.py:34
  619.7 55.0 %gather_fusion.1 = bf16[20224,3,128]{2,1,0:T(4,128)(2,1)} fusion(bf16[3,4609,128]{2,0,1:T(4,128)(2,1)} %get-tuple-element.348, s32[20480]{0:T(1024)S(1)} %pad_clamp_fusion.6), kind=kCustom, calls=%fused_computation.1.clone.clone.1 | custom fusion | bytes 31144960 | tf_op jit(solution)/shard_map/while/body/eval_jaxpr/while/body/eval_jaxpr/jit(_take)/gather | solution.py:29
  674.7 11.4 %fusion.52 = f32[3,256,128]{2,1,0:T(8,128)S(1)} fusion(bf16[4,79,128,128]{3,2,1,0:T(8,128)(2,1)} %get-tuple-element.349, s32[]{:T(128)} %get-tuple-element.338, bf16[3,79,256,128]{3,0,2,1:T(4,128)(2,1)} %bitcast.177, pred[79,256]{1,0:T(8,128)(4,1)S(1)} %compare_and_fusion.5, f32[3,256,128]{2,1,0:T(8,128)S(1)} %get-tuple-element.339, pred[]{:T(512)S(6)} %compare.7), kind=kOutput, calls=%fused_computation.26.clone.1 | convolution fusion | flops 1996062720 | bytes 24105216 | tf_op jit(solution)/shard_map/while/body/eval_jaxpr/while/body/eval_jaxpr/ktbp,tqp->kbq/dot_general | solution.py:34
  687.5 166.4 %while.41 = (s32[]{:T(128)}, f32[3,64,128]{2,1,0:T(8,128)S(1)}, s32[4,79,64]{1,0,2:T(4,128)}, bf16[3,577,128]{2,0,1:T(4,128)(2,1)S(1)}, bf16[4,79,128,128]{3,2,1,0:T(8,128)(2,1)}, /*index=5*/s32[]{:T(128)}, s32[]{:T(128)}) while((s32[]{:T(128)}, f32[3,64,128]{2,1,0:T(8,128)S(1)}, s32[4,79,64]{1,0,2:T(4,128)}, ...), condition=%wide.region_1.2_spmd.clone, body=%wide.region_0.1_spmd.clone.sunk | while | flops 499066304 | bytes 15982299 | solution.py:40
  688.7 35.6 %gather_fusion = bf16[5056,3,128]{2,1,0:T(4,128)(2,1)} fusion(bf16[3,577,128]{2,0,1:T(4,128)(2,1)S(1)} %get-tuple-element.396, s32[5120]{0:T(1024)S(1)} %pad_clamp_fusion.5), kind=kCustom, calls=%fused_computation.clone.clone.1 | custom fusion | bytes 7786240 | tf_op jit(solution)/shard_map/while/body/eval_jaxpr/while/body/eval_jaxpr/jit(_take)/gather | solution.py:29
  724.3 4.8 fusion.49
  730.3 35.6 %gather_fusion = bf16[5056,3,128]{2,1,0:T(4,128)(2,1)} fusion(bf16[3,577,128]{2,0,1:T(4,128)(2,1)S(1)} %get-tuple-element.396, s32[5120]{0:T(1024)S(1)} %pad_clamp_fusion.5), kind=kCustom, calls=%fused_computation.clone.clone.1 | custom fusion | bytes 7786240 | tf_op jit(solution)/shard_map/while/body/eval_jaxpr/while/body/eval_jaxpr/jit(_take)/gather | solution.py:29
  765.9 4.8 fusion.49
  771.9 35.6 %gather_fusion = bf16[5056,3,128]{2,1,0:T(4,128)(2,1)} fusion(bf16[3,577,128]{2,0,1:T(4,128)(2,1)S(1)} %get-tuple-element.396, s32[5120]{0:T(1024)S(1)} %pad_clamp_fusion.5), kind=kCustom, calls=%fused_computation.clone.clone.1 | custom fusion | bytes 7786240 | tf_op jit(solution)/shard_map/while/body/eval_jaxpr/while/body/eval_jaxpr/jit(_take)/gather | solution.py:29
  807.5 4.8 fusion.49
  813.5 35.6 %gather_fusion = bf16[5056,3,128]{2,1,0:T(4,128)(2,1)} fusion(bf16[3,577,128]{2,0,1:T(4,128)(2,1)S(1)} %get-tuple-element.396, s32[5120]{0:T(1024)S(1)} %pad_clamp_fusion.5), kind=kCustom, calls=%fused_computation.clone.clone.1 | custom fusion | bytes 7786240 | tf_op jit(solution)/shard_map/while/body/eval_jaxpr/while/body/eval_jaxpr/jit(_take)/gather | solution.py:29
  849.1 4.8 fusion.49
  (152 shorter events, 29.7 us)
Async XLA Ops:
  0.0 853.9 %copy-start = (bf16[8,128,128]{2,1,0:T(8,128)(2,1)S(1)}, bf16[8,128,128]{2,1,0:T(8,128)(2,1)}, u32[]{:S(2)}) copy-start(bf16[8,128,128]{2,1,0:T(8,128)(2,1)} %param.18) | copy-start | bytes 786436
  38.5 22.6 %copy-start.1 = (bf16[512,3,128]{2,0,1:T(8,128)(2,1)S(1)}, bf16[512,3,128]{2,0,1:T(8,128)(2,1)}, u32[]{:S(2)}) copy-start(bf16[512,3,128]{2,0,1:T(8,128)(2,1)} %param.15) | copy-start | bytes 1179652
  38.5 22.6 %copy-start.10 = (bf16[8,128,128]{2,1,0:T(8,128)(2,1)S(1)}, bf16[8,128,128]{2,1,0:T(8,128)(2,1)}, u32[]{:S(2)}) copy-start(bf16[8,128,128]{2,1,0:T(8,128)(2,1)} %param.16) | copy-start | bytes 786436
  38.5 23.0 %copy-start.9 = (s32[1,16,32]{2,1,0:T(8,128)S(1)}, s32[1,16,32]{2,1,0:T(8,128)}, u32[]{:S(2)}) copy-start(s32[1,16,32]{2,1,0:T(8,128)} %param.23) | copy-start | bytes 6148
  42.1 34.6 %collective-permute-start = (bf16[256,3,128]{2,0,1:T(8,128)(2,1)}, bf16[256,3,128]{2,0,1:T(8,128)(2,1)}, u32[]{:S(2)}, u32[]{:S(2)}) collective-permute-start(bf16[256,3,128]{2,0,1:T(8,128)(2,1)} %get-tuple-element.224), channel_id=1, source_target_pairs={{0,1},{1,2},{2,3},{3,4},{4,5},{5,6},{6,7},{7,8},{8,9},{9,10},{10,1... | collective-permute-start | bytes 589832 | tf_op jit(solution)/shard_map/ppermute | solution.py:10
  45.3 38.0 %collective-permute-start.1 = (bf16[256,3,128]{2,0,1:T(8,128)(2,1)}, bf16[256,3,128]{2,0,1:T(8,128)(2,1)}, u32[]{:S(2)}, u32[]{:S(2)}) collective-permute-start(bf16[256,3,128]{2,0,1:T(8,128)(2,1)} %get-tuple-element.223), channel_id=1, source_target_pairs={{0,2},{1,3},{2,4},{3,5},{4,6},{5,7},{6,8},{7,9},{8,10},{9,11},{10,... | collective-permute-start | bytes 589832 | tf_op jit(solution)/shard_map/ppermute | solution.py:10
  49.9 38.7 %collective-permute-start.2 = (bf16[256,3,128]{2,0,1:T(8,128)(2,1)}, bf16[256,3,128]{2,0,1:T(8,128)(2,1)}, u32[]{:S(2)}, u32[]{:S(2)}) collective-permute-start(bf16[256,3,128]{2,0,1:T(8,128)(2,1)} %get-tuple-element.222), channel_id=1, source_target_pairs={{0,3},{1,4},{2,5},{3,6},{4,7},{5,8},{6,9},{7,10},{8,11},{9,12},{10... | collective-permute-start | bytes 589832 | tf_op jit(solution)/shard_map/ppermute | solution.py:10
  54.2 38.2 %collective-permute-start.3 = (bf16[256,3,128]{2,0,1:T(8,128)(2,1)}, bf16[256,3,128]{2,0,1:T(8,128)(2,1)}, u32[]{:S(2)}, u32[]{:S(2)}) collective-permute-start(bf16[256,3,128]{2,0,1:T(8,128)(2,1)} %get-tuple-element.221), channel_id=1, source_target_pairs={{0,4},{1,5},{2,6},{3,7},{4,8},{5,9},{6,10},{7,11},{8,12},{9,13},{1... | collective-permute-start | bytes 589832 | tf_op jit(solution)/shard_map/ppermute | solution.py:10
  57.8 39.3 %collective-permute-start.4 = (bf16[256,3,128]{2,0,1:T(8,128)(2,1)}, bf16[256,3,128]{2,0,1:T(8,128)(2,1)}, u32[]{:S(2)}, u32[]{:S(2)}) collective-permute-start(bf16[256,3,128]{2,0,1:T(8,128)(2,1)} %get-tuple-element.220), channel_id=1, source_target_pairs={{0,5},{1,6},{2,7},{3,8},{4,9},{5,10},{6,11},{7,12},{8,13},{9,14},{... | collective-permute-start | bytes 589832 | tf_op jit(solution)/shard_map/ppermute | solution.py:10
  61.4 0.6 copy-start.3
  65.0 621.2 %all-to-all-start = ((bf16[16,32,3,128]{3,1,2,0:T(8,128)(2,1)}), bf16[16,32,3,128]{3,1,2,0:T(8,128)(2,1)}, u32[]{:S(2)}, u32[]{:S(2)}) async-start(bf16[16,32,3,128]{3,1,2,0:T(8,128)(2,1)} %copy.52), calls=%async_computation | async-start | bytes 786432 | tf_op jit(solution)/shard_map/all_to_all | solution.py:84
  73.4 40.3 %copy-start.2 = (bf16[256,3,128]{2,0,1:T(8,128)(2,1)S(1)}, bf16[256,3,128]{2,0,1:T(8,128)(2,1)}, u32[]{:S(2)}) copy-start(bf16[256,3,128]{2,0,1:T(8,128)(2,1)} %get-tuple-element.211) | copy-start | bytes 589828
  76.8 25.0 %collective-permute-start.5 = (bf16[256,3,128]{2,0,1:T(8,128)(2,1)}, bf16[256,3,128]{2,0,1:T(8,128)(2,1)S(1)}, u32[]{:S(2)}, u32[]{:S(2)}) collective-permute-start(bf16[256,3,128]{2,0,1:T(8,128)(2,1)} %get-tuple-element.219), channel_id=1, source_target_pairs={{0,6},{1,7},{2,8},{3,9},{4,10},{5,11},{6,12},{7,13},{8,14},{9,15},... | collective-permute-start | bytes 589832 | tf_op jit(solution)/shard_map/ppermute | solution.py:10
  83.3 22.1 %collective-permute-start.6 = (bf16[256,3,128]{2,0,1:T(8,128)(2,1)}, bf16[256,3,128]{2,0,1:T(8,128)(2,1)S(1)}, u32[]{:S(2)}, u32[]{:S(2)}) collective-permute-start(bf16[256,3,128]{2,0,1:T(8,128)(2,1)} %get-tuple-element.218), channel_id=1, source_target_pairs={{0,7},{1,8},{2,9},{3,10},{4,11},{5,12},{6,13},{7,14},{8,15},{9,16}... | collective-permute-start | bytes 589832 | tf_op jit(solution)/shard_map/ppermute | solution.py:10
  88.6 19.9 %collective-permute-start.7 = (bf16[256,3,128]{2,0,1:T(8,128)(2,1)}, bf16[256,3,128]{2,0,1:T(8,128)(2,1)S(1)}, u32[]{:S(2)}, u32[]{:S(2)}) collective-permute-start(bf16[256,3,128]{2,0,1:T(8,128)(2,1)} %get-tuple-element.217), channel_id=1, source_target_pairs={{0,8},{1,9},{2,10},{3,11},{4,12},{5,13},{6,14},{7,15},{8,16},{9,17... | collective-permute-start | bytes 589832 | tf_op jit(solution)/shard_map/ppermute | solution.py:10
  92.4 21.3 %collective-permute-start.8 = (bf16[256,3,128]{2,0,1:T(8,128)(2,1)}, bf16[256,3,128]{2,0,1:T(8,128)(2,1)S(1)}, u32[]{:S(2)}, u32[]{:S(2)}) collective-permute-start(bf16[256,3,128]{2,0,1:T(8,128)(2,1)} %get-tuple-element.216), channel_id=1, source_target_pairs={{1,0},{2,1},{3,2},{4,3},{5,4},{6,5},{7,6},{8,7},{9,8},{10,9},{11,1... | collective-permute-start | bytes 589832 | tf_op jit(solution)/shard_map/ppermute | solution.py:10
  97.1 20.4 %collective-permute-start.9 = (bf16[256,3,128]{2,0,1:T(8,128)(2,1)}, bf16[256,3,128]{2,0,1:T(8,128)(2,1)S(1)}, u32[]{:S(2)}, u32[]{:S(2)}) collective-permute-start(bf16[256,3,128]{2,0,1:T(8,128)(2,1)} %get-tuple-element.215), channel_id=1, source_target_pairs={{2,0},{3,1},{4,2},{5,3},{6,4},{7,5},{8,6},{9,7},{10,8},{11,9},{12,... | collective-permute-start | bytes 589832 | tf_op jit(solution)/shard_map/ppermute | solution.py:10
  101.7 18.1 %collective-permute-start.10 = (bf16[256,3,128]{2,0,1:T(8,128)(2,1)}, bf16[256,3,128]{2,0,1:T(8,128)(2,1)S(1)}, u32[]{:S(2)}, u32[]{:S(2)}) collective-permute-start(bf16[256,3,128]{2,0,1:T(8,128)(2,1)} %get-tuple-element.214), channel_id=1, source_target_pairs={{3,0},{4,1},{5,2},{6,3},{7,4},{8,5},{9,6},{10,7},{11,8},{12,9},{13... | collective-permute-start | bytes 589832 | tf_op jit(solution)/shard_map/ppermute | solution.py:10
  105.4 18.4 %collective-permute-start.11 = (bf16[256,3,128]{2,0,1:T(8,128)(2,1)}, bf16[256,3,128]{2,0,1:T(8,128)(2,1)S(1)}, u32[]{:S(2)}, u32[]{:S(2)}) collective-permute-start(bf16[256,3,128]{2,0,1:T(8,128)(2,1)} %get-tuple-element.213), channel_id=1, source_target_pairs={{4,0},{5,1},{6,2},{7,3},{8,4},{9,5},{10,6},{11,7},{12,8},{13,9},{1... | collective-permute-start | bytes 589832 | tf_op jit(solution)/shard_map/ppermute | solution.py:10
  108.5 15.4 %collective-permute-start.12 = (bf16[256,3,128]{2,0,1:T(8,128)(2,1)}, bf16[256,3,128]{2,0,1:T(8,128)(2,1)S(1)}, u32[]{:S(2)}, u32[]{:S(2)}) collective-permute-start(bf16[256,3,128]{2,0,1:T(8,128)(2,1)} %get-tuple-element.212), channel_id=1, source_target_pairs={{5,0},{6,1},{7,2},{8,3},{9,4},{10,5},{11,6},{12,7},{13,8},{14,9},{... | collective-permute-start | bytes 589832 | tf_op jit(solution)/shard_map/ppermute | solution.py:10
  113.7 10.2 %collective-permute-start.13 = (bf16[256,3,128]{2,0,1:T(8,128)(2,1)S(1)}, bf16[256,3,128]{2,0,1:T(8,128)(2,1)S(1)}, u32[]{:S(2)}, u32[]{:S(2)}) collective-permute-start(bf16[256,3,128]{2,0,1:T(8,128)(2,1)S(1)} %copy-done.2), channel_id=1, source_target_pairs={{6,0},{7,1},{8,2},{9,3},{10,4},{11,5},{12,6},{13,7},{14,8},{15,9},... | collective-permute-start | bytes 589832 | tf_op jit(solution)/shard_map/ppermute | solution.py:10
  117.5 11.4 %collective-permute-start.14 = (bf16[256,3,128]{2,0,1:T(8,128)(2,1)S(1)}, bf16[256,3,128]{2,0,1:T(8,128)(2,1)S(1)}, u32[]{:S(2)}, u32[]{:S(2)}) collective-permute-start(bf16[256,3,128]{2,0,1:T(8,128)(2,1)S(1)} %get-tuple-element.210), channel_id=1, source_target_pairs={{7,0},{8,1},{9,2},{10,3},{11,4},{12,5},{13,6},{14,7},{15,8},{16,9}... | collective-permute-start | bytes 589832 | tf_op jit(solution)/shard_map/ppermute | solution.py:10
  119.8 9.1 %collective-permute-start.15 = (bf16[256,3,128]{2,0,1:T(8,128)(2,1)S(1)}, bf16[256,3,128]{2,0,1:T(8,128)(2,1)S(1)}, u32[]{:S(2)}, u32[]{:S(2)}) collective-permute-start(bf16[256,3,128]{2,0,1:T(8,128)(2,1)S(1)} %get-tuple-element.209), channel_id=1, source_target_pairs={{8,0},{9,1},{10,2},{11,3},{12,4},{13,5},{14,6},{15,7},{16,8},{17,9... | collective-permute-start | bytes 589832 | tf_op jit(solution)/shard_map/ppermute | solution.py:10
  129.3 2.4 copy-start.7
  151.0 536.2 %copy-start.4 = (bf16[64,3,128]{2,0,1:T(8,128)(2,1)S(1)}, bf16[64,3,128]{2,0,1:T(8,128)(2,1)}, u32[]{:S(2)}) copy-start(bf16[64,3,128]{2,0,1:T(8,128)(2,1)} %copy-done.3) | copy-start | bytes 147460
  151.0 536.2 %copy-start.8 = (bf16[1,3,128]{2,0,1:T(2,128)(2,1)S(1)}, bf16[1,3,128]{2,0,1:T(2,128)(2,1)}, u32[]{:S(2)}) copy-start(bf16[1,3,128]{2,0,1:T(2,128)(2,1)} %copy-done.7) | copy-start | bytes 2308
  151.0 536.5 %copy-start.6 = (f32[3,64,128]{2,1,0:T(8,128)S(1)}, f32[3,64,128]{2,1,0:T(8,128)}, u32[]{:S(2)}) copy-start(f32[3,64,128]{2,1,0:T(8,128)} %custom-call.1) | copy-start | bytes 294916
  687.5 166.4 %copy-start.5 = (bf16[128,128]{1,0:T(8,128)(2,1)S(1)}, bf16[128,128]{1,0:T(8,128)(2,1)}, u32[]{:S(2)}) copy-start(bf16[128,128]{1,0:T(8,128)(2,1)} %param.19) | copy-start | bytes 98308
where the time goes:
time: 862 us; the launch traced here: 856 us
  local copies, waits for them, and re-layouts  660 us (77%)
  matrix products  112 us (13%)
  starting transfers between devices  69.3 us (8%)
    gather x12, local copies, waits for them, and re-layouts, step(): jnp.take(planes, picked.reshape(-1), axis=1)  582 us
    dot_general x12, matrix products, step(): jnp.einsum('ktbp,tqp->kbq', gathered, operators, preferred_element_type=j...  110 us
    ppermute x16, starting transfers between devices, from_behind(): lax.ppermute(value, axis, [(source, source + steps) for source in range(f...  60.8 us
    gather x1, local copies, waits for them, and re-layouts, local(): outgoing = leaf_up[leaf_ghosts[0]]  37.7 us
    while x1, local copies, waits for them, and re-layouts, translate(): result = lax.map(per_block, chosen)  19.3 us
  transfers between devices with their start and end apart: 17, of which 1 were waited for; matrix products, arithmetic and copies ran while one was open for 66% of the time, Pallas kernels for 0%

commit v1 on v0

v1 whole, which is shorter than its diff:
```python
import jax
import jax.numpy as jnp
from jax import lax
from jax.experimental import pallas as pl
from jax.experimental.pallas import tpu as pltpu
from jax.sharding import PartitionSpec as P

RING = 4
VMEM_BYTES = 58 * 2**20


def dot_nt(left, right):
    return lax.dot_general(
        left, right, (((1,), (1,)), ((), ())), preferred_element_type=jnp.float32
    )


def pick_pair(table, low_half, first, second):
    upper = table[pl.ds(first + 4, 8), :]
    lower = table[pl.ds(second, 8), :]
    return jnp.where(low_half, upper, lower)


def prepare_kernel(
    planes_ref, ghosts_ref, parent_ghosts_ref, operators_ref, *refs, offsets, slots, columns, parent_slots
):
    outgoing = refs[:offsets]
    parent_ref, parent_sent_ref, table, parent_table, gathered, parent_gathered = refs[offsets:]
    boxes = planes_ref.shape[1]
    parents = parent_ref.shape[1]
    low_half = lax.broadcasted_iota(jnp.int32, (8, 128), 0) < 4
    for k in range(3):
        table[pl.ds(4 + k, boxes, stride=4), :] = planes_ref[k].astype(jnp.float32)
    operators = jnp.concatenate([operators_ref[c] for c in range(8)], axis=1)
    for k in range(3):
        children = jnp.concatenate(
            [table[pl.ds(4 + 4 * c + k, parents, stride=32), :] for c in range(8)], axis=1
        ).astype(jnp.bfloat16)
        rounded = dot_nt(children, operators).astype(jnp.bfloat16)
        parent_ref[k] = rounded
        parent_table[pl.ds(4 + k, parents, stride=4), :] = rounded.astype(jnp.float32)
    for column in range(columns):
        for pair in range(parent_slots // 2):
            at = column * parent_slots + 2 * pair
            parent_gathered[8 * pair : 8 * pair + 8, :] = pick_pair(
                parent_table, low_half, parent_ghosts_ref[0, at], parent_ghosts_ref[0, at + 1]
            )
        for k in range(3):
            parent_sent_ref[column, k] = parent_gathered[
                pl.ds(k, parent_slots, stride=4), :
            ].astype(jnp.bfloat16)
    for which in range(offsets):
        for pair in range(slots // 2):
            at = which * slots + 2 * pair
            gathered[8 * pair : 8 * pair + 8, :] = pick_pair(
                table, low_half, ghosts_ref[0, at], ghosts_ref[0, at + 1]
            )
        for k in range(3):
            outgoing[which][k] = gathered[pl.ds(k, slots, stride=4), :].astype(jnp.bfloat16)


def prepare(planes, ghosts, parent_ghosts, operators):
    boxes = planes.shape[1]
    parents = boxes // 8
    offsets, slots = ghosts.shape
    columns, parent_slots = parent_ghosts.shape
    vmem = pl.BlockSpec(memory_space=pltpu.VMEM)
    smem = pl.BlockSpec(memory_space=pltpu.SMEM)

    def kernel(*refs):
        prepare_kernel(
            *refs, offsets=offsets, slots=slots, columns=columns, parent_slots=parent_slots
        )

    out = pl.pallas_call(
        kernel,
        in_specs=[vmem, smem, smem, vmem],
        out_specs=[vmem] * (offsets + 2),
        out_shape=[jax.ShapeDtypeStruct((3, slots, 128), jnp.bfloat16)] * offsets
        + [
            jax.ShapeDtypeStruct((3, parents, 128), jnp.bfloat16),
            jax.ShapeDtypeStruct((columns, 3, parent_slots, 128), jnp.bfloat16),
        ],
        scratch_shapes=[
            pltpu.VMEM((4 * boxes + 16, 128), jnp.float32),
            pltpu.VMEM((4 * parents + 16, 128), jnp.float32),
            pltpu.VMEM((4 * slots, 128), jnp.float32),
            pltpu.VMEM((4 * parent_slots, 128), jnp.float32),
        ],
        compiler_params=pltpu.CompilerParams(vmem_limit_bytes=VMEM_BYTES),
        name="prepare",
    )(
        planes,
        (ghosts * 4).reshape(1, -1),
        (parent_ghosts * 4).reshape(1, -1),
        operators,
    )
    return out[:offsets], out[offsets], out[offsets + 1]


def order_lists(lists, block, group):
    boxes, vectors = lists.shape
    places = (lists + 1) * 4
    places = places.T.reshape(vectors // group, group, boxes // block, block)
    places = places.transpose(0, 2, 1, 3).reshape(-1, 1, group * block)
    steps = places.shape[0]
    padding = -steps % RING + RING
    return jnp.concatenate(
        [places, jnp.zeros((padding, 1, group * block), places.dtype)], axis=0
    )


def translate_steps(lists_hbm, table, operators, total, chunk, chunk_sem, block, group):
    blocks = total.shape[0]
    groups = operators.shape[0] // group
    steps = lists_hbm.shape[0] - RING
    low_half = lax.broadcasted_iota(jnp.int32, (8, 128), 0) < 4

    def fetch(step, slot):
        return pltpu.make_async_copy(lists_hbm.at[step], chunk.at[slot], chunk_sem.at[slot])

    def round_of_steps(turn, _):
        for slot in range(RING):
            step = turn * RING + slot
            fetch(step, slot).wait()
            which = jnp.minimum(step // blocks, groups - 1)
            target = step % blocks
            columns = []
            for t in range(group):
                rows = []
                for pair in range(block // 2):
                    at = t * block + 2 * pair
                    rows.append(
                        pick_pair(table, low_half, chunk[slot, 0, at], chunk[slot, 0, at + 1])
                    )
                columns.append(jnp.concatenate(rows, axis=0).astype(jnp.bfloat16))
            sources = jnp.concatenate(columns, axis=1)
            matrices = jnp.concatenate(
                [operators[which * group + t] for t in range(group)], axis=1
            )
            total[target] += dot_nt(sources, matrices)
            fetch(step + RING, slot).start()
        return 0

    lax.fori_loop(0, steps // RING, round_of_steps, 0)
    for slot in range(RING):
        fetch(steps + slot, slot).wait()


def first_fetches(lists_hbm, chunk, chunk_sem):
    for slot in range(RING):
        pltpu.make_async_copy(lists_hbm.at[slot], chunk.at[slot], chunk_sem.at[slot]).start()


def parent_level(own, came, lists, translations, inverse, block, group):
    parents = own.shape[1]
    columns, _, slots, _ = came.shape
    count = parents + columns * slots

    def kernel(
        own_ref, came_ref, lists_hbm, operators_ref, inverse_ref, out_ref,
        table, total, result, chunk, chunk_sem,
    ):
        first_fetches(lists_hbm, chunk, chunk_sem)
        table[...] = jnp.zeros_like(table)
        total[...] = jnp.zeros_like(total)
        for k in range(3):
            table[pl.ds(8 + k, parents, stride=4), :] = own_ref[k].astype(jnp.float32)
            for column in range(columns):
                at = 8 + k + 4 * (parents + column * slots)
                table[pl.ds(at, slots, stride=4), :] = came_ref[column, k].astype(jnp.float32)
        translate_steps(
            lists_hbm, table, operators_ref, total, chunk, chunk_sem, block, group
        )
        check = total[...].reshape(4 * parents, 128).astype(jnp.bfloat16)
        result[...] = dot_nt(check, inverse_ref[...])
        for k in range(3):
            out_ref[k] = result[pl.ds(k, parents, stride=4), :].astype(jnp.bfloat16)

    vmem = pl.BlockSpec(memory_space=pltpu.VMEM)
    hbm = pl.BlockSpec(memory_space=pl.ANY)
    return pl.pallas_call(
        kernel,
        in_specs=[vmem, vmem, hbm, vmem, vmem],
        out_specs=vmem,
        out_shape=jax.ShapeDtypeStruct((3, parents, 128), jnp.bfloat16),
        scratch_shapes=[
            pltpu.VMEM((4 * count + 16, 128), jnp.float32),
            pltpu.VMEM((parents // block, 4 * block, 128), jnp.float32),
            pltpu.VMEM((4 * parents, 128), jnp.float32),
            pltpu.SMEM((RING, 1, block * group), jnp.int32),
            pltpu.SemaphoreType.DMA((RING,)),
        ],
        compiler_params=pltpu.CompilerParams(vmem_limit_bytes=VMEM_BYTES),
        name="parent_level",
    )(own, came, lists, translations, inverse)


def leaf_level(own, arrived, parent_down, lists, translations, to_child, inverse, block, group):
    boxes = own.shape[1]
    parents = boxes // 8
    offsets = len(arrived)
    slots = arrived[0].shape[1]
    count = boxes + offsets * slots

    def kernel(*refs):
        own_ref, parent_ref, lists_hbm, operators_hbm, to_child_ref, inverse_ref = refs[:6]
        ghost_hbm = refs[6 : 6 + offsets]
        (
            out_ref, table, operators, ghosts, total, result, chunk, chunk_sem, operator_sem,
            ghost_sem,
        ) = refs[6 + offsets :]
        ghost_copies = [
            pltpu.make_async_copy(ghost_hbm[j], ghosts.at[j], ghost_sem.at[j])
            for j in range(offsets)
        ]
        for copy in ghost_copies:
            copy.start()
        operator_copy = pltpu.make_async_copy(operators_hbm, operators, operator_sem)
        operator_copy.start()
        first_fetches(lists_hbm, chunk, chunk_sem)
        low_rows = jnp.zeros((8, 128), jnp.float32)
        table[0:8, :] = low_rows
        table[pl.ds(8 + 3, count, stride=4), :] = jnp.zeros((count, 128), jnp.float32)
        for k in range(3):
            table[pl.ds(8 + k, boxes, stride=4), :] = own_ref[k].astype(jnp.float32)
        result[...] = jnp.zeros_like(result)
        for c in range(8):
            for k in range(3):
                result[pl.ds(4 * c + k, parents, stride=32), :] = dot_nt(
                    parent_ref[k], to_child_ref[c]
                )
        for b in range(boxes // block):
            total[b] = result[4 * block * b : 4 * block * (b + 1), :]
        for j in range(offsets):
            ghost_copies[j].wait()
            for k in range(3):
                at = 8 + k + 4 * (boxes + j * slots)
                table[pl.ds(at, slots, stride=4), :] = ghosts[j, k].astype(jnp.float32)
        operator_copy.wait()
        translate_steps(lists_hbm, table, operators, total, chunk, chunk_sem, block, group)
        for b in range(boxes // block):
            result[4 * block * b : 4 * block * (b + 1), :] = dot_nt(
                total[b].astype(jnp.bfloat16), inverse_ref[...]
            )
        for k in range(3):
            out_ref[k] = result[pl.ds(k, boxes, stride=4), :].astype(jnp.bfloat16)

    vmem = pl.BlockSpec(memory_space=pltpu.VMEM)
    hbm = pl.BlockSpec(memory_space=pl.ANY)
    return pl.pallas_call(
        kernel,
        in_specs=[vmem, vmem, hbm, hbm, vmem, vmem] + [hbm] * offsets,
        out_specs=vmem,
        out_shape=jax.ShapeDtypeStruct((3, boxes, 128), jnp.bfloat16),
        scratch_shapes=[
            pltpu.VMEM((4 * count + 16, 128), jnp.float32),
            pltpu.VMEM(translations.shape, translations.dtype),
            pltpu.VMEM((offsets, 3, slots, 128), jnp.bfloat16),
            pltpu.VMEM((boxes // block, 4 * block, 128), jnp.float32),
            pltpu.VMEM((4 * boxes, 128), jnp.float32),
            pltpu.SMEM((RING, 1, block * group), jnp.int32),
            pltpu.SemaphoreType.DMA((RING,)),
            pltpu.SemaphoreType.DMA,
            pltpu.SemaphoreType.DMA((offsets,)),
        ],
        compiler_params=pltpu.CompilerParams(vmem_limit_bytes=VMEM_BYTES),
        name="leaf_level",
    )(own, parent_down, lists, translations, to_child, inverse, *arrived)


def from_behind(value, axis, steps):
    count = lax.axis_size(axis)
    first, last = (max(0, -steps), min(count, count - steps))
    return lax.ppermute(value, axis, [(source, source + steps) for source in range(first, last)])


def rank_distance(which, near_count):
    if which < near_count:
        return which + 1
    return -(which - near_count + 1)


def local(
    leaf_up,
    child_to_parent,
    translations,
    parent_to_child,
    check_to_density,
    leaf_lists,
    leaf_ghosts,
    parent_lists,
    parent_ghosts,
):
    planes = leaf_up.transpose(1, 0, 2)
    outgoing, parent_up, parent_sent = prepare(
        planes, leaf_ghosts[0], parent_ghosts[0], child_to_parent
    )
    near_count = len(outgoing) // 2
    parent_came = lax.all_to_all(parent_sent, "col", split_axis=0, concat_axis=0, tiled=True)
    arrived = [None] * len(outgoing)
    for distance in range(near_count):
        for which in (distance, distance + near_count):
            arrived[which] = from_behind(
                outgoing[which], ("row", "col"), rank_distance(which, near_count)
            )
    parent_down = parent_level(
        parent_up,
        parent_came,
        order_lists(parent_lists, 64, 4),
        translations,
        check_to_density,
        64,
        4,
    )
    leaf_down = leaf_level(
        planes,
        arrived,
        parent_down,
        order_lists(leaf_lists, 128, 4),
        translations,
        parent_to_child,
        check_to_density,
        128,
        4,
    )
    return leaf_down.transpose(1, 0, 2)


def solution(mesh):
    return jax.shard_map(
        local,
        mesh=mesh,
        in_specs=(
            P(("row", "col"), None, None),
            P(),
            P(),
            P(),
            P(),
            P(("row", "col"), None),
            P(("row", "col"), None, None),
            P(("row", "col"), None),
            P(("row", "col"), None, None),
        ),
        out_specs=P(("row", "col"), None, None),
        check_vma=False,
    )
```

time: 862 us -> 267 us (0.31)
  local copies, waits for them, and re-layouts: 660 us -> 5.37 us
  Pallas kernels: 0 us -> 179 us
  matrix products: 112 us -> 0 us
    gather x15 -> x0, local copies, waits for them, and re-layouts: 623 us -> none  [the longest x12 582 us: step(): jnp.take(planes, picked.reshape(-1), axis=1)]
    pallas_call x0 -> x3, Pallas kernels: none -> 179 us  [the longest x1 147 us: leaf_level(): pl.pallas_call(kernel, in_specs=[vmem, vmem, hbm, hbm, vmem, vmem] + [hbm...]
    dot_general x15 -> x0, matrix products: 112 us -> none  [the longest x12 110 us: step(): jnp.einsum('ktbp,tqp->kbq', gathered, operators, preferred_element_type=j...]
    while x17 -> x0, local copies, waits for them, and re-layouts: 20.1 us -> none  [the longest x1 19.3 us: translate(): result = lax.map(per_block, chosen)]
  transfers between devices with their start and end apart: 17 -> 17, of which waited for: 1 -> 1; matrix products, arithmetic and copies ran while one was open for 66% -> 2% of each run, Pallas kernels for 0% -> 10%
where the time goes in v1:
time: 267 us; the launch traced here: 266 us
  Pallas kernels  179 us (67%)
  starting transfers between devices  72.1 us (27%)
  waiting for transfers between devices  5.61 us (2%)
  local copies, waits for them, and re-layouts  5.37 us (2%)
  other arithmetic  3.49 us (1%)
    pallas_call x1, Pallas kernels, leaf_level(): pl.pallas_call(kernel, in_specs=[vmem, vmem, hbm, hbm, vmem, vmem] + [hbm...  147 us
    ppermute x16, starting transfers between devices, from_behind(): lax.ppermute(value, axis, [(source, source + steps) for source in range(f...  66.6 us
    pallas_call x1, Pallas kernels, parent_level(): pl.pallas_call(kernel, in_specs=[vmem, vmem, hbm, vmem, vmem], out_specs=...  25.4 us
    pallas_call x1, Pallas kernels, prepare(): pl.pallas_call(kernel, in_specs=[vmem, smem, smem, vmem], out_specs=[vmem...  6.07 us
    ppermute x16, waiting for transfers between devices, from_behind(): lax.ppermute(value, axis, [(source, source + steps) for source in range(f...  5.6 us
    all_to_all x1, starting transfers between devices, local(): lax.all_to_all(parent_sent, 'col', split_axis=0, concat_axis=0, tiled=True)  5.41 us
  transfers between devices with their start and end apart: 17, of which 1 were waited for; matrix products, arithmetic and copies ran while one was open for 2% of the time, Pallas kernels for 10%

profile of v1, /device:TPU:3, one launch (start us, length us, event | category | flops | bytes accessed | tf_op | source)
XLA Modules:
  0.0 265.6 jit_solution(6576381424976088623)
XLA Ops:
  0.0 0.7 multiply_bitcast_fusion.2
  0.7 0.6 copy.15
  1.3 0.7 broadcast_multiply_fusion
  2.0 0.7 mul.49.refs_2_
  2.7 6.1 %prepare.1 = (bf16[3,256,128]{2,1,0:T(8,128)(2,1)}, bf16[3,256,128]{2,1,0:T(8,128)(2,1)}, bf16[3,256,128]{2,1,0:T(8,128)(2,1)}, bf16[3,256,128]{2,1,0:T(8,128)(2...) custom-call(bf16[3,512,128]{2,1,0:T(8,128)(2,1)} %bitcast.13, ...), custom_call_target="tpu_custom_call" | custom-call | tf_op jit(solution)/shard_map/prepare/pallas_call | solution.py:75
  8.8 3.2 %collective-permute-start = (bf16[3,256,128]{2,1,0:T(8,128)(2,1)}, bf16[3,256,128]{2,1,0:T(8,128)(2,1)S(1)}, u32[]{:S(2)}, u32[]{:S(2)}) collective-permute-start(bf16[3,256,128]{2,1,0:T(8,128)(2,1)} %get-tuple-element.25), channel_id=1, source_target_pairs={{0,1},{1,2},{2,3},{3,4},{4,5},{5,6},{6,7},{7,8},{8,9},{9,10},{10,1... | collective-permute-start | bytes 589832 | tf_op jit(solution)/shard_map/ppermute | solution.py:275
  12.0 4.5 %collective-permute-start.1 = (bf16[3,256,128]{2,1,0:T(8,128)(2,1)}, bf16[3,256,128]{2,1,0:T(8,128)(2,1)S(1)}, u32[]{:S(2)}, u32[]{:S(2)}) collective-permute-start(bf16[3,256,128]{2,1,0:T(8,128)(2,1)} %get-tuple-element.26), channel_id=1, source_target_pairs={{0,2},{1,3},{2,4},{3,5},{4,6},{5,7},{6,8},{7,9},{8,10},{9,11},{10,... | collective-permute-start | bytes 589832 | tf_op jit(solution)/shard_map/ppermute | solution.py:275
  16.5 5.6 %collective-permute-start.10 = (bf16[3,256,128]{2,1,0:T(8,128)(2,1)}, bf16[3,256,128]{2,1,0:T(8,128)(2,1)S(1)}, u32[]{:S(2)}, u32[]{:S(2)}) collective-permute-start(bf16[3,256,128]{2,1,0:T(8,128)(2,1)} %get-tuple-element.35), channel_id=1, source_target_pairs={{3,0},{4,1},{5,2},{6,3},{7,4},{8,5},{9,6},{10,7},{11,8},{12,9},{13... | collective-permute-start | bytes 589832 | tf_op jit(solution)/shard_map/ppermute | solution.py:275
  22.1 3.6 %collective-permute-start.11 = (bf16[3,256,128]{2,1,0:T(8,128)(2,1)}, bf16[3,256,128]{2,1,0:T(8,128)(2,1)S(1)}, u32[]{:S(2)}, u32[]{:S(2)}) collective-permute-start(bf16[3,256,128]{2,1,0:T(8,128)(2,1)} %get-tuple-element.36), channel_id=1, source_target_pairs={{4,0},{5,1},{6,2},{7,3},{8,4},{9,5},{10,6},{11,7},{12,8},{13,9},{1... | collective-permute-start | bytes 589832 | tf_op jit(solution)/shard_map/ppermute | solution.py:275
  25.7 4.0 %collective-permute-start.12 = (bf16[3,256,128]{2,1,0:T(8,128)(2,1)}, bf16[3,256,128]{2,1,0:T(8,128)(2,1)S(1)}, u32[]{:S(2)}, u32[]{:S(2)}) collective-permute-start(bf16[3,256,128]{2,1,0:T(8,128)(2,1)} %get-tuple-element.37), channel_id=1, source_target_pairs={{5,0},{6,1},{7,2},{8,3},{9,4},{10,5},{11,6},{12,7},{13,8},{14,9},{... | collective-permute-start | bytes 589832 | tf_op jit(solution)/shard_map/ppermute | solution.py:275
  29.7 0.0 collective-permute-done.refs_6_
  29.8 3.6 %collective-permute-start.13 = (bf16[3,256,128]{2,1,0:T(8,128)(2,1)}, bf16[3,256,128]{2,1,0:T(8,128)(2,1)S(1)}, u32[]{:S(2)}, u32[]{:S(2)}) collective-permute-start(bf16[3,256,128]{2,1,0:T(8,128)(2,1)} %get-tuple-element.38), channel_id=1, source_target_pairs={{6,0},{7,1},{8,2},{9,3},{10,4},{11,5},{12,6},{13,7},{14,8},{15,9},... | collective-permute-start | bytes 589832 | tf_op jit(solution)/shard_map/ppermute | solution.py:275
  33.4 5.4 %all-to-all-start = ((bf16[16,3,32,128]{3,2,1,0:T(8,128)(2,1)}), bf16[16,3,32,128]{3,2,1,0:T(8,128)(2,1)S(1)}, u32[]{:S(2)}, u32[]{:S(2)}) async-start(bf16[16,3,32,128]{3,2,1,0:T(8,128)(2,1)} %get-tuple-element.24), calls=%async_computation | async-start | bytes 786432 | tf_op jit(solution)/shard_map/all_to_all | solution.py:300
  38.8 0.0 collective-permute-done.1.refs_7_
  38.8 5.7 %collective-permute-start.14 = (bf16[3,256,128]{2,1,0:T(8,128)(2,1)}, bf16[3,256,128]{2,1,0:T(8,128)(2,1)S(1)}, u32[]{:S(2)}, u32[]{:S(2)}) collective-permute-start(bf16[3,256,128]{2,1,0:T(8,128)(2,1)} %get-tuple-element.39), channel_id=1, source_target_pairs={{7,0},{8,1},{9,2},{10,3},{11,4},{12,5},{13,6},{14,7},{15,8},{16,9}... | collective-permute-start | bytes 589832 | tf_op jit(solution)/shard_map/ppermute | solution.py:275
  44.5 0.0 collective-permute-done.10.refs_16_
  44.5 2.5 collective-permute-start.15
  47.0 0.0 collective-permute-done.11.refs_17_
  47.0 3.4 %collective-permute-start.2 = (bf16[3,256,128]{2,1,0:T(8,128)(2,1)}, bf16[3,256,128]{2,1,0:T(8,128)(2,1)S(1)}, u32[]{:S(2)}, u32[]{:S(2)}) collective-permute-start(bf16[3,256,128]{2,1,0:T(8,128)(2,1)} %get-tuple-element.27), channel_id=1, source_target_pairs={{0,3},{1,4},{2,5},{3,6},{4,7},{5,8},{6,9},{7,10},{8,11},{9,12},{10... | collective-permute-start | bytes 589832 | tf_op jit(solution)/shard_map/ppermute | solution.py:275
  50.4 0.0 collective-permute-done.12.refs_18_
  50.4 2.5 collective-permute-start.3
  52.9 0.0 collective-permute-done.13.refs_19_
  53.0 3.7 %collective-permute-start.4 = (bf16[3,256,128]{2,1,0:T(8,128)(2,1)}, bf16[3,256,128]{2,1,0:T(8,128)(2,1)S(1)}, u32[]{:S(2)}, u32[]{:S(2)}) collective-permute-start(bf16[3,256,128]{2,1,0:T(8,128)(2,1)} %get-tuple-element.29), channel_id=1, source_target_pairs={{0,5},{1,6},{2,7},{3,8},{4,9},{5,10},{6,11},{7,12},{8,13},{9,14},{... | collective-permute-start | bytes 589832 | tf_op jit(solution)/shard_map/ppermute | solution.py:275
  56.7 0.9 multiply_bitcast_fusion.1
  57.6 0.1 copy.12
  57.7 0.1 reshape_transpose_reshape.4
  57.8 0.0 collective-permute-done.14.refs_20_
  57.8 5.5 %collective-permute-start.5 = (bf16[3,256,128]{2,1,0:T(8,128)(2,1)}, bf16[3,256,128]{2,1,0:T(8,128)(2,1)}, u32[]{:S(2)}, u32[]{:S(2)}) collective-permute-start(bf16[3,256,128]{2,1,0:T(8,128)(2,1)} %get-tuple-element.30), channel_id=1, source_target_pairs={{0,6},{1,7},{2,8},{3,9},{4,10},{5,11},{6,12},{7,13},{8,14},{9,15},... | collective-permute-start | bytes 589832 | tf_op jit(solution)/shard_map/ppermute | solution.py:275
  63.4 0.0 collective-permute-done.15.refs_21_
  63.4 5.7 %collective-permute-start.6 = (bf16[3,256,128]{2,1,0:T(8,128)(2,1)}, bf16[3,256,128]{2,1,0:T(8,128)(2,1)}, u32[]{:S(2)}, u32[]{:S(2)}) collective-permute-start(bf16[3,256,128]{2,1,0:T(8,128)(2,1)} %get-tuple-element.31), channel_id=1, source_target_pairs={{0,7},{1,8},{2,9},{3,10},{4,11},{5,12},{6,13},{7,14},{8,15},{9,16}... | collective-permute-start | bytes 589832 | tf_op jit(solution)/shard_map/ppermute | solution.py:275
  69.1 0.0 collective-permute-done.2.refs_8_
  69.1 3.4 %collective-permute-start.7 = (bf16[3,256,128]{2,1,0:T(8,128)(2,1)}, bf16[3,256,128]{2,1,0:T(8,128)(2,1)}, u32[]{:S(2)}, u32[]{:S(2)}) collective-permute-start(bf16[3,256,128]{2,1,0:T(8,128)(2,1)} %get-tuple-element.32), channel_id=1, source_target_pairs={{0,8},{1,9},{2,10},{3,11},{4,12},{5,13},{6,14},{7,15},{8,16},{9,17... | collective-permute-start | bytes 589832 | tf_op jit(solution)/shard_map/ppermute | solution.py:275
  72.5 5.6 %collective-permute-done.3.refs_9_ = bf16[3,256,128]{2,1,0:T(8,128)(2,1)S(1)} collective-permute-done((bf16[3,256,128]{2,1,0:T(8,128)(2,1)}, bf16[3,256,128]{2,1,0:T(8,128)(2,1)S(1)}, u32[]{:S(2)}, u32[]{:S(2)}) %collective-permute-start.3) | collective-permute-done | bytes 196640 | tf_op jit(solution)/shard_map/ppermute | solution.py:275
  78.1 1.9 collective-permute-start.8
  80.0 0.0 collective-permute-done.4.refs_10_
  80.1 0.7 copy-done.11
  80.7 7.8 %collective-permute-start.9 = (bf16[3,256,128]{2,1,0:T(8,128)(2,1)}, bf16[3,256,128]{2,1,0:T(8,128)(2,1)}, u32[]{:S(2)}, u32[]{:S(2)}) collective-permute-start(bf16[3,256,128]{2,1,0:T(8,128)(2,1)} %get-tuple-element.34), channel_id=1, source_target_pairs={{2,0},{3,1},{4,2},{5,3},{6,4},{7,5},{8,6},{9,7},{10,8},{11,9},{12,... | collective-permute-start | bytes 589832 | tf_op jit(solution)/shard_map/ppermute | solution.py:275
  88.6 1.2 multiply_bitcast_fusion
  89.8 0.2 reshape.32
  90.0 0.2 copy.14
  90.2 0.7 concatenate.6.lists_hbm
  90.9 1.3 concatenate.7.refs_2_
  92.2 0.0 all-to-all-done.came_ref
  92.2 0.7 copy-done
  92.9 25.4 %parent_level.1.refs_1_ = bf16[3,64,128]{2,1,0:T(8,128)(2,1)} custom-call(bf16[3,64,128]{2,1,0:T(8,128)(2,1)} %get-tuple-element.23.own_ref, bf16[16,3,32,128]{3,2,1,0:T(8,128)(2,1)} %copy-done, s32[84,1,256]{2,1,0:T(1,128)} %concatenate.6.lists_hbm, bf16[316,128,128]{2,1,0:T(8,128)(2,1)} %refs_3_.3, bf16[128,128]{1,0:T(8,128)(2,1)} %refs_5_.1), custom_call_target="tpu_custom_call" | custom-call | tf_op jit(solution)/shard_map/parent_level/pallas_call | solution.py:182
  118.4 0.0 collective-permute-done.6.refs_12_
  118.4 0.0 collective-permute-done.7.refs_13_
  118.5 147.1 %leaf_level.1 = bf16[3,512,128]{2,1,0:T(8,128)(2,1)} custom-call(bf16[3,512,128]{2,1,0:T(8,128)(2,1)} %bitcast.14, bf16[3,64,128]{2,1,0:T(8,128)(2,1)} %parent_level.1.refs_1_, s32[320,1,512]{2,1,0:T(1,128)} %concatenate.7.refs_2_, bf16[316,128,128]{2,1,0:T(8,128)(2,1)} %refs_3_.3, bf16[8,128,128]{2,1,0:T(8,128)(2,1)} %refs_4_.1, bf16[128,128]{1,0:T(8,128)(2,1)} %refs_5_.1, ...), custom_call_target="tpu_custom_call" | custom-call | tf_op jit(solution)/shard_map/leaf_level/pallas_call | solution.py:251
  (25 shorter events, 0.1 us)
Async XLA Ops:
  8.8 21.0 %collective-permute-start = (bf16[3,256,128]{2,1,0:T(8,128)(2,1)}, bf16[3,256,128]{2,1,0:T(8,128)(2,1)S(1)}, u32[]{:S(2)}, u32[]{:S(2)}) collective-permute-start(bf16[3,256,128]{2,1,0:T(8,128)(2,1)} %get-tuple-element.25), channel_id=1, source_target_pairs={{0,1},{1,2},{2,3},{3,4},{4,5},{5,6},{6,7},{7,8},{8,9},{9,10},{10,1... | collective-permute-start | bytes 589832 | tf_op jit(solution)/shard_map/ppermute | solution.py:275
  12.0 26.8 %collective-permute-start.1 = (bf16[3,256,128]{2,1,0:T(8,128)(2,1)}, bf16[3,256,128]{2,1,0:T(8,128)(2,1)S(1)}, u32[]{:S(2)}, u32[]{:S(2)}) collective-permute-start(bf16[3,256,128]{2,1,0:T(8,128)(2,1)} %get-tuple-element.26), channel_id=1, source_target_pairs={{0,2},{1,3},{2,4},{3,5},{4,6},{5,7},{6,8},{7,9},{8,10},{9,11},{10,... | collective-permute-start | bytes 589832 | tf_op jit(solution)/shard_map/ppermute | solution.py:275
  16.5 28.0 %collective-permute-start.10 = (bf16[3,256,128]{2,1,0:T(8,128)(2,1)}, bf16[3,256,128]{2,1,0:T(8,128)(2,1)S(1)}, u32[]{:S(2)}, u32[]{:S(2)}) collective-permute-start(bf16[3,256,128]{2,1,0:T(8,128)(2,1)} %get-tuple-element.35), channel_id=1, source_target_pairs={{3,0},{4,1},{5,2},{6,3},{7,4},{8,5},{9,6},{10,7},{11,8},{12,9},{13... | collective-permute-start | bytes 589832 | tf_op jit(solution)/shard_map/ppermute | solution.py:275
  22.1 24.8 %collective-permute-start.11 = (bf16[3,256,128]{2,1,0:T(8,128)(2,1)}, bf16[3,256,128]{2,1,0:T(8,128)(2,1)S(1)}, u32[]{:S(2)}, u32[]{:S(2)}) collective-permute-start(bf16[3,256,128]{2,1,0:T(8,128)(2,1)} %get-tuple-element.36), channel_id=1, source_target_pairs={{4,0},{5,1},{6,2},{7,3},{8,4},{9,5},{10,6},{11,7},{12,8},{13,9},{1... | collective-permute-start | bytes 589832 | tf_op jit(solution)/shard_map/ppermute | solution.py:275
  25.7 24.7 %collective-permute-start.12 = (bf16[3,256,128]{2,1,0:T(8,128)(2,1)}, bf16[3,256,128]{2,1,0:T(8,128)(2,1)S(1)}, u32[]{:S(2)}, u32[]{:S(2)}) collective-permute-start(bf16[3,256,128]{2,1,0:T(8,128)(2,1)} %get-tuple-element.37), channel_id=1, source_target_pairs={{5,0},{6,1},{7,2},{8,3},{9,4},{10,5},{11,6},{12,7},{13,8},{14,9},{... | collective-permute-start | bytes 589832 | tf_op jit(solution)/shard_map/ppermute | solution.py:275
  29.8 88.6 %copy-start.1 = (bf16[3,256,128]{2,1,0:T(8,128)(2,1)}, bf16[3,256,128]{2,1,0:T(8,128)(2,1)S(1)}, u32[]{:S(2)}) copy-start(bf16[3,256,128]{2,1,0:T(8,128)(2,1)S(1)} %collective-permute-done.refs_6_) | copy-start | bytes 589828
  29.8 23.2 %collective-permute-start.13 = (bf16[3,256,128]{2,1,0:T(8,128)(2,1)}, bf16[3,256,128]{2,1,0:T(8,128)(2,1)S(1)}, u32[]{:S(2)}, u32[]{:S(2)}) collective-permute-start(bf16[3,256,128]{2,1,0:T(8,128)(2,1)} %get-tuple-element.38), channel_id=1, source_target_pairs={{6,0},{7,1},{8,2},{9,3},{10,4},{11,5},{12,6},{13,7},{14,8},{15,9},... | collective-permute-start | bytes 589832 | tf_op jit(solution)/shard_map/ppermute | solution.py:275
  33.4 58.8 %all-to-all-start = ((bf16[16,3,32,128]{3,2,1,0:T(8,128)(2,1)}), bf16[16,3,32,128]{3,2,1,0:T(8,128)(2,1)S(1)}, u32[]{:S(2)}, u32[]{:S(2)}) async-start(bf16[16,3,32,128]{3,2,1,0:T(8,128)(2,1)} %get-tuple-element.24), calls=%async_computation | async-start | bytes 786432 | tf_op jit(solution)/shard_map/all_to_all | solution.py:300
  38.8 79.6 %copy-start.2 = (bf16[3,256,128]{2,1,0:T(8,128)(2,1)}, bf16[3,256,128]{2,1,0:T(8,128)(2,1)S(1)}, u32[]{:S(2)}) copy-start(bf16[3,256,128]{2,1,0:T(8,128)(2,1)S(1)} %collective-permute-done.1.refs_7_) | copy-start | bytes 589828
  38.8 19.0 %collective-permute-start.14 = (bf16[3,256,128]{2,1,0:T(8,128)(2,1)}, bf16[3,256,128]{2,1,0:T(8,128)(2,1)S(1)}, u32[]{:S(2)}, u32[]{:S(2)}) collective-permute-start(bf16[3,256,128]{2,1,0:T(8,128)(2,1)} %get-tuple-element.39), channel_id=1, source_target_pairs={{7,0},{8,1},{9,2},{10,3},{11,4},{12,5},{13,6},{14,7},{15,8},{16,9}... | collective-permute-start | bytes 589832 | tf_op jit(solution)/shard_map/ppermute | solution.py:275
  44.5 73.9 %copy-start.3 = (bf16[3,256,128]{2,1,0:T(8,128)(2,1)}, bf16[3,256,128]{2,1,0:T(8,128)(2,1)S(1)}, u32[]{:S(2)}) copy-start(bf16[3,256,128]{2,1,0:T(8,128)(2,1)S(1)} %collective-permute-done.10.refs_16_) | copy-start | bytes 589828
  44.5 18.9 %collective-permute-start.15 = (bf16[3,256,128]{2,1,0:T(8,128)(2,1)}, bf16[3,256,128]{2,1,0:T(8,128)(2,1)S(1)}, u32[]{:S(2)}, u32[]{:S(2)}) collective-permute-start(bf16[3,256,128]{2,1,0:T(8,128)(2,1)} %get-tuple-element.40), channel_id=1, source_target_pairs={{8,0},{9,1},{10,2},{11,3},{12,4},{13,5},{14,6},{15,7},{16,8},{17,9... | collective-permute-start | bytes 589832 | tf_op jit(solution)/shard_map/ppermute | solution.py:275
  47.0 71.5 %copy-start.4 = (bf16[3,256,128]{2,1,0:T(8,128)(2,1)}, bf16[3,256,128]{2,1,0:T(8,128)(2,1)S(1)}, u32[]{:S(2)}) copy-start(bf16[3,256,128]{2,1,0:T(8,128)(2,1)S(1)} %collective-permute-done.11.refs_17_) | copy-start | bytes 589828
  47.0 22.1 %collective-permute-start.2 = (bf16[3,256,128]{2,1,0:T(8,128)(2,1)}, bf16[3,256,128]{2,1,0:T(8,128)(2,1)S(1)}, u32[]{:S(2)}, u32[]{:S(2)}) collective-permute-start(bf16[3,256,128]{2,1,0:T(8,128)(2,1)} %get-tuple-element.27), channel_id=1, source_target_pairs={{0,3},{1,4},{2,5},{3,6},{4,7},{5,8},{6,9},{7,10},{8,11},{9,12},{10... | collective-permute-start | bytes 589832 | tf_op jit(solution)/shard_map/ppermute | solution.py:275
  50.4 68.0 %copy-start.5 = (bf16[3,256,128]{2,1,0:T(8,128)(2,1)}, bf16[3,256,128]{2,1,0:T(8,128)(2,1)S(1)}, u32[]{:S(2)}) copy-start(bf16[3,256,128]{2,1,0:T(8,128)(2,1)S(1)} %collective-permute-done.12.refs_18_) | copy-start | bytes 589828
  50.4 27.7 %collective-permute-start.3 = (bf16[3,256,128]{2,1,0:T(8,128)(2,1)}, bf16[3,256,128]{2,1,0:T(8,128)(2,1)S(1)}, u32[]{:S(2)}, u32[]{:S(2)}) collective-permute-start(bf16[3,256,128]{2,1,0:T(8,128)(2,1)} %get-tuple-element.28), channel_id=1, source_target_pairs={{0,4},{1,5},{2,6},{3,7},{4,8},{5,9},{6,10},{7,11},{8,12},{9,13},{1... | collective-permute-start | bytes 589832 | tf_op jit(solution)/shard_map/ppermute | solution.py:275
  53.0 65.5 %copy-start.6 = (bf16[3,256,128]{2,1,0:T(8,128)(2,1)}, bf16[3,256,128]{2,1,0:T(8,128)(2,1)S(1)}, u32[]{:S(2)}) copy-start(bf16[3,256,128]{2,1,0:T(8,128)(2,1)S(1)} %collective-permute-done.13.refs_19_) | copy-start | bytes 589828
  53.0 27.1 %collective-permute-start.4 = (bf16[3,256,128]{2,1,0:T(8,128)(2,1)}, bf16[3,256,128]{2,1,0:T(8,128)(2,1)S(1)}, u32[]{:S(2)}, u32[]{:S(2)}) collective-permute-start(bf16[3,256,128]{2,1,0:T(8,128)(2,1)} %get-tuple-element.29), channel_id=1, source_target_pairs={{0,5},{1,6},{2,7},{3,8},{4,9},{5,10},{6,11},{7,12},{8,13},{9,14},{... | collective-permute-start | bytes 589832 | tf_op jit(solution)/shard_map/ppermute | solution.py:275
  57.8 60.6 %copy-start.7 = (bf16[3,256,128]{2,1,0:T(8,128)(2,1)}, bf16[3,256,128]{2,1,0:T(8,128)(2,1)S(1)}, u32[]{:S(2)}) copy-start(bf16[3,256,128]{2,1,0:T(8,128)(2,1)S(1)} %collective-permute-done.14.refs_20_) | copy-start | bytes 589828
  57.8 60.5 %collective-permute-start.5 = (bf16[3,256,128]{2,1,0:T(8,128)(2,1)}, bf16[3,256,128]{2,1,0:T(8,128)(2,1)}, u32[]{:S(2)}, u32[]{:S(2)}) collective-permute-start(bf16[3,256,128]{2,1,0:T(8,128)(2,1)} %get-tuple-element.30), channel_id=1, source_target_pairs={{0,6},{1,7},{2,8},{3,9},{4,10},{5,11},{6,12},{7,13},{8,14},{9,15},... | collective-permute-start | bytes 589832 | tf_op jit(solution)/shard_map/ppermute | solution.py:275
  63.4 55.1 %copy-start.8 = (bf16[3,256,128]{2,1,0:T(8,128)(2,1)}, bf16[3,256,128]{2,1,0:T(8,128)(2,1)S(1)}, u32[]{:S(2)}) copy-start(bf16[3,256,128]{2,1,0:T(8,128)(2,1)S(1)} %collective-permute-done.15.refs_21_) | copy-start | bytes 589828
  63.4 55.0 %collective-permute-start.6 = (bf16[3,256,128]{2,1,0:T(8,128)(2,1)}, bf16[3,256,128]{2,1,0:T(8,128)(2,1)}, u32[]{:S(2)}, u32[]{:S(2)}) collective-permute-start(bf16[3,256,128]{2,1,0:T(8,128)(2,1)} %get-tuple-element.31), channel_id=1, source_target_pairs={{0,7},{1,8},{2,9},{3,10},{4,11},{5,12},{6,13},{7,14},{8,15},{9,16}... | collective-permute-start | bytes 589832 | tf_op jit(solution)/shard_map/ppermute | solution.py:275
  69.1 49.4 %copy-start.9 = (bf16[3,256,128]{2,1,0:T(8,128)(2,1)}, bf16[3,256,128]{2,1,0:T(8,128)(2,1)S(1)}, u32[]{:S(2)}) copy-start(bf16[3,256,128]{2,1,0:T(8,128)(2,1)S(1)} %collective-permute-done.2.refs_8_) | copy-start | bytes 589828
  69.1 49.2 %collective-permute-start.7 = (bf16[3,256,128]{2,1,0:T(8,128)(2,1)}, bf16[3,256,128]{2,1,0:T(8,128)(2,1)}, u32[]{:S(2)}, u32[]{:S(2)}) collective-permute-start(bf16[3,256,128]{2,1,0:T(8,128)(2,1)} %get-tuple-element.32), channel_id=1, source_target_pairs={{0,8},{1,9},{2,10},{3,11},{4,12},{5,13},{6,14},{7,15},{8,16},{9,17... | collective-permute-start | bytes 589832 | tf_op jit(solution)/shard_map/ppermute | solution.py:275
  78.1 1.9 copy-start.10
  78.1 40.3 %collective-permute-start.8 = (bf16[3,256,128]{2,1,0:T(8,128)(2,1)}, bf16[3,256,128]{2,1,0:T(8,128)(2,1)}, u32[]{:S(2)}, u32[]{:S(2)}) collective-permute-start(bf16[3,256,128]{2,1,0:T(8,128)(2,1)} %get-tuple-element.33), channel_id=1, source_target_pairs={{1,0},{2,1},{3,2},{4,3},{5,4},{6,5},{7,6},{8,7},{9,8},{10,9},{11,1... | collective-permute-start | bytes 589832 | tf_op jit(solution)/shard_map/ppermute | solution.py:275
  80.0 0.7 copy-start.11
  80.7 37.7 %collective-permute-start.9 = (bf16[3,256,128]{2,1,0:T(8,128)(2,1)}, bf16[3,256,128]{2,1,0:T(8,128)(2,1)}, u32[]{:S(2)}, u32[]{:S(2)}) collective-permute-start(bf16[3,256,128]{2,1,0:T(8,128)(2,1)} %get-tuple-element.34), channel_id=1, source_target_pairs={{2,0},{3,1},{4,2},{5,3},{6,4},{7,5},{8,6},{9,7},{10,8},{11,9},{12,... | collective-permute-start | bytes 589832 | tf_op jit(solution)/shard_map/ppermute | solution.py:275
  92.2 0.7 copy-start

commit v2 on v1

v2 whole, which is shorter than its diff:
```python
import jax
import jax.numpy as jnp
from jax import lax
from jax.experimental import pallas as pl
from jax.experimental.pallas import tpu as pltpu
from jax.sharding import PartitionSpec as P

RING = 2
NEAR = 8
VMEM_BYTES = 58 * 2**20


def dot_nt(left, right):
    return lax.dot_general(
        left, right, (((1,), (1,)), ((), ())), preferred_element_type=jnp.float32
    )


def pick_pair(table, low_half, first, second):
    upper = table[pl.ds(first + 4, 8), :]
    lower = table[pl.ds(second, 8), :]
    return jnp.where(low_half, upper, lower)


def spread(table, at, planes_ref):
    for k in range(3):
        plane = planes_ref[k]
        table[pl.ds(at + k, plane.shape[0], stride=4), :] = plane.astype(jnp.float32)


def select_rows(table, places_ref, start, count, gathered, out_ref):
    low_half = lax.broadcasted_iota(jnp.int32, (8, 128), 0) < 4
    for pair in range(count // 2):
        at = start + 2 * pair
        gathered[8 * pair : 8 * pair + 8, :] = pick_pair(
            table, low_half, places_ref[0, at], places_ref[0, at + 1]
        )
    for k in range(3):
        out_ref[k] = gathered[pl.ds(k, count, stride=4), :].astype(jnp.bfloat16)


def raise_parents(planes, ghosts, operators):
    boxes = planes.shape[1]
    parents = boxes // 8
    columns, slots = ghosts.shape

    def kernel(
        planes_ref, ghosts_ref, operators_ref, up_ref, sent_ref, zero_ref, table, own, gathered
    ):
        zero_ref[0, 0] = 0
        spread(table, 0, planes_ref)
        matrices = jnp.concatenate([operators_ref[c] for c in range(8)], axis=1)
        for k in range(3):
            children = jnp.concatenate(
                [table[pl.ds(4 * c + k, parents, stride=32), :] for c in range(8)], axis=1
            )
            up_ref[k] = dot_nt(children.astype(jnp.bfloat16), matrices).astype(jnp.bfloat16)
        spread(own, 4, up_ref)
        for column in range(columns):
            select_rows(own, ghosts_ref, column * slots, slots, gathered, sent_ref.at[column])

    vmem = pl.BlockSpec(memory_space=pltpu.VMEM)
    return pl.pallas_call(
        kernel,
        in_specs=[vmem, pl.BlockSpec(memory_space=pltpu.SMEM), vmem],
        out_specs=[vmem, vmem, pl.BlockSpec(memory_space=pltpu.SMEM)],
        out_shape=[
            jax.ShapeDtypeStruct((3, parents, 128), jnp.bfloat16),
            jax.ShapeDtypeStruct((columns, 3, slots, 128), jnp.bfloat16),
            jax.ShapeDtypeStruct((1, 1), jnp.int32),
        ],
        scratch_shapes=[
            pltpu.VMEM((4 * boxes, 128), jnp.float32),
            pltpu.VMEM((4 * parents + 16, 128), jnp.float32),
            pltpu.VMEM((4 * slots, 128), jnp.float32),
        ],
        compiler_params=pltpu.CompilerParams(vmem_limit_bytes=VMEM_BYTES),
        name="raise_parents",
    )(planes, (ghosts * 4).reshape(1, -1), operators)


def select_leaves(planes, ghosts):
    boxes = planes.shape[1]
    messages, slots = ghosts.shape

    def kernel(planes_ref, ghosts_ref, sent_ref, direct_ref, table, gathered):
        spread(table, 4, planes_ref)
        for which in range(messages):
            target = direct_ref if which == messages - 1 else sent_ref.at[which]
            select_rows(table, ghosts_ref, which * slots, slots, gathered, target)

    vmem = pl.BlockSpec(memory_space=pltpu.VMEM)
    return pl.pallas_call(
        kernel,
        in_specs=[vmem, pl.BlockSpec(memory_space=pltpu.SMEM)],
        out_specs=[vmem, vmem],
        out_shape=[
            jax.ShapeDtypeStruct((messages - 1, 3, slots, 128), jnp.bfloat16),
            jax.ShapeDtypeStruct((3, slots, 128), jnp.bfloat16),
        ],
        scratch_shapes=[
            pltpu.VMEM((4 * boxes + 16, 128), jnp.float32),
            pltpu.VMEM((4 * slots, 128), jnp.float32),
        ],
        compiler_params=pltpu.CompilerParams(vmem_limit_bytes=VMEM_BYTES),
        name="select_leaves",
    )(planes, (ghosts * 4).reshape(1, -1))


def order_lists(lists, block, group, chunk_steps):
    boxes, vectors = lists.shape
    places = (lists + 1) * 4
    places = places.T.reshape(vectors // group, group, boxes // block, block)
    places = places.transpose(0, 2, 1, 3).reshape(-1, group * block)
    padding = -places.shape[0] % (RING * chunk_steps) + RING * chunk_steps
    places = jnp.concatenate(
        [places, jnp.zeros((padding, group * block), places.dtype)], axis=0
    )
    return places.reshape(-1, 1, chunk_steps * group * block)


def translate_steps(
    lists_hbm, table, operators, total, chunk, chunk_sem, block, group, chunk_steps, at_turn
):
    blocks = total.shape[0]
    groups = operators.shape[0] // group
    chunks = lists_hbm.shape[0] - RING
    size = block * group
    low_half = lax.broadcasted_iota(jnp.int32, (8, 128), 0) < 4

    def fetch(at, slot):
        return pltpu.make_async_copy(lists_hbm.at[at], chunk.at[slot], chunk_sem.at[slot])

    def round_of_chunks(turn, _):
        at_turn(turn)
        for slot in range(RING):
            fetch(turn * RING + slot, slot).wait()
            for h in range(chunk_steps):
                which = ((turn * RING + slot) * chunk_steps + h) // blocks
                which = jnp.minimum(which, groups - 1)
                columns = []
                for t in range(group):
                    rows = []
                    for pair in range(block // 2):
                        at = h * size + t * block + 2 * pair
                        rows.append(
                            pick_pair(table, low_half, chunk[slot, 0, at], chunk[slot, 0, at + 1])
                        )
                    columns.append(jnp.concatenate(rows, axis=0).astype(jnp.bfloat16))
                sources = jnp.concatenate(columns, axis=1)
                matrices = jnp.concatenate(
                    [operators[which * group + t] for t in range(group)], axis=1
                )
                total[h % blocks] += dot_nt(sources, matrices)
            fetch((turn + 1) * RING + slot, slot).start()
        return 0

    lax.fori_loop(0, chunks // RING, round_of_chunks, 0)
    for slot in range(RING):
        fetch(chunks + slot, slot).wait()


def split_operator_copy(operators_hbm, operators, sems, first):
    return (
        pltpu.make_async_copy(
            operators_hbm.at[pl.ds(0, first)], operators.at[pl.ds(0, first)], sems.at[0]
        ),
        pltpu.make_async_copy(
            operators_hbm.at[pl.ds(first, operators.shape[0] - first)],
            operators.at[pl.ds(first, operators.shape[0] - first)],
            sems.at[1],
        ),
    )


def first_fetches(lists_hbm, chunk, chunk_sem):
    for slot in range(RING):
        pltpu.make_async_copy(lists_hbm.at[slot], chunk.at[slot], chunk_sem.at[slot]).start()


def parent_level(own, came, lists, translations, inverse, block, group, chunk_steps):
    parents = own.shape[1]
    columns, _, slots, _ = came.shape
    count = parents + columns * slots
    first = RING * chunk_steps * group

    def kernel(
        own_ref, came_ref, lists_hbm, operators_hbm, inverse_ref, out_ref,
        table, operators, total, result, chunk, chunk_sem, operator_sem,
    ):
        early, late = split_operator_copy(operators_hbm, operators, operator_sem, first)
        early.start()
        first_fetches(lists_hbm, chunk, chunk_sem)
        late.start()
        table[...] = jnp.zeros_like(table)
        total[...] = jnp.zeros_like(total)
        spread(table, 8, own_ref)
        for column in range(columns):
            spread(table, 8 + 4 * (parents + column * slots), came_ref.at[column])
        early.wait()

        def at_turn(turn):
            pl.when(turn == 1)(lambda: late.wait())

        translate_steps(
            lists_hbm, table, operators, total, chunk, chunk_sem, block, group, chunk_steps,
            at_turn,
        )
        check = total[...].reshape(4 * parents, 128).astype(jnp.bfloat16)
        result[...] = dot_nt(check, inverse_ref[...])
        for k in range(3):
            out_ref[k] = result[pl.ds(k, parents, stride=4), :].astype(jnp.bfloat16)

    vmem = pl.BlockSpec(memory_space=pltpu.VMEM)
    hbm = pl.BlockSpec(memory_space=pl.ANY)
    return pl.pallas_call(
        kernel,
        in_specs=[vmem, vmem, hbm, hbm, vmem],
        out_specs=vmem,
        out_shape=jax.ShapeDtypeStruct((3, parents, 128), jnp.bfloat16),
        scratch_shapes=[
            pltpu.VMEM((4 * count + 16, 128), jnp.float32),
            pltpu.VMEM(translations.shape, translations.dtype),
            pltpu.VMEM((parents // block, 4 * block, 128), jnp.float32),
            pltpu.VMEM((4 * parents, 128), jnp.float32),
            pltpu.SMEM((RING, 1, chunk_steps * block * group), jnp.int32),
            pltpu.SemaphoreType.DMA((RING,)),
            pltpu.SemaphoreType.DMA((2,)),
        ],
        compiler_params=pltpu.CompilerParams(vmem_limit_bytes=VMEM_BYTES),
        name="parent_level",
    )(own, came, lists, translations, inverse)


def leaf_level(
    own, came, shifted, direct, origin, parent_down, lists, translations, to_child, inverse,
    block, group, chunk_steps,
):
    boxes = own.shape[1]
    parents = boxes // 8
    offsets = origin.shape[1]
    slots = direct.shape[1]
    count = boxes + offsets * slots
    first = RING * chunk_steps * group // (boxes // block)

    def kernel(
        origin_ref, own_ref, parent_ref, to_child_ref, inverse_ref, lists_hbm, operators_hbm,
        came_hbm, shifted_hbm, direct_hbm, out_ref,
        table, operators, ghosts, total, result, chunk, chunk_sem, operator_sem, ghost_sem,
    ):
        def ghost_copy(source, j):
            return pltpu.make_async_copy(source, ghosts.at[j], ghost_sem.at[j])

        for j in range(offsets):
            kind, place = origin_ref[0, j], origin_ref[1, j]
            pl.when(kind == 0)(lambda: ghost_copy(came_hbm.at[place], j).start())
            pl.when(kind == 1)(lambda: ghost_copy(shifted_hbm.at[place], j).start())
            pl.when(kind == 2)(lambda: ghost_copy(direct_hbm, j).start())
        first_fetches(lists_hbm, chunk, chunk_sem)
        early, late = split_operator_copy(operators_hbm, operators, operator_sem, first)
        early.start()
        late.start()
        table[0:8, :] = jnp.zeros((8, 128), jnp.float32)
        table[pl.ds(8 + 3, count, stride=4), :] = jnp.zeros((count, 128), jnp.float32)
        spread(table, 8, own_ref)
        result[pl.ds(3, boxes, stride=4), :] = jnp.zeros((boxes, 128), jnp.float32)
        for c in range(8):
            for k in range(3):
                result[pl.ds(4 * c + k, parents, stride=32), :] = dot_nt(
                    parent_ref[k], to_child_ref[c]
                )
        for b in range(boxes // block):
            total[b] = result[4 * block * b : 4 * block * (b + 1), :]
        for j in range(offsets):
            ghost_copy(direct_hbm, j).wait()
            spread(table, 8 + 4 * (boxes + j * slots), ghosts.at[j])
        early.wait()

        def at_turn(turn):
            pl.when(turn == 1)(lambda: late.wait())

        translate_steps(
            lists_hbm, table, operators, total, chunk, chunk_sem, block, group, chunk_steps,
            at_turn,
        )
        for b in range(boxes // block):
            result[4 * block * b : 4 * block * (b + 1), :] = dot_nt(
                total[b].astype(jnp.bfloat16), inverse_ref[...]
            )
        for k in range(3):
            out_ref[k] = result[pl.ds(k, boxes, stride=4), :].astype(jnp.bfloat16)

    vmem = pl.BlockSpec(memory_space=pltpu.VMEM)
    smem = pl.BlockSpec(memory_space=pltpu.SMEM)
    hbm = pl.BlockSpec(memory_space=pl.ANY)
    return pl.pallas_call(
        kernel,
        in_specs=[smem, vmem, vmem, vmem, vmem, hbm, hbm, hbm, hbm, hbm],
        out_specs=vmem,
        out_shape=jax.ShapeDtypeStruct((3, boxes, 128), jnp.bfloat16),
        scratch_shapes=[
            pltpu.VMEM((4 * count + 16, 128), jnp.float32),
            pltpu.VMEM(translations.shape, translations.dtype),
            pltpu.VMEM((offsets, 3, slots, 128), jnp.bfloat16),
            pltpu.VMEM((boxes // block, 4 * block, 128), jnp.float32),
            pltpu.VMEM((4 * boxes, 128), jnp.float32),
            pltpu.SMEM((RING, 1, chunk_steps * block * group), jnp.int32),
            pltpu.SemaphoreType.DMA((RING,)),
            pltpu.SemaphoreType.DMA((2,)),
            pltpu.SemaphoreType.DMA((offsets,)),
        ],
        compiler_params=pltpu.CompilerParams(vmem_limit_bytes=VMEM_BYTES),
        name="leaf_level",
    )(
        origin, own, parent_down, to_child, inverse, lists, translations, came, shifted, direct
    )


def offset_index(distance):
    return jnp.where(distance > 0, distance - 1, NEAR - 1 - distance)


def message_order(column, columns):
    difference = jnp.arange(columns) - column
    distance = jnp.where(difference > NEAR, difference - columns, difference)
    distance = jnp.where(distance < -NEAR, distance + columns, distance)
    order = jnp.where(distance == 0, 0, offset_index(distance))
    last = offset_index(jnp.where(column < NEAR, -NEAR, NEAR))
    return jnp.concatenate([order, last[None]])


def message_origin(column, columns):
    offset = jnp.arange(2 * NEAR)
    distance = jnp.where(offset < NEAR, offset + 1, NEAR - 1 - offset)
    sender = column - distance
    inside = (sender >= 0) & (sender < columns)
    direct = jnp.abs(distance) == NEAR
    kind = jnp.where(inside, 0, jnp.where(direct, 2, 1))
    turned = jnp.where(sender < 0, sender + NEAR - 1, sender - columns)
    place = jnp.where(inside, sender, jnp.where(direct, 0, turned))
    return jnp.stack([kind, place]).astype(jnp.int32)


def local(
    leaf_up,
    child_to_parent,
    translations,
    parent_to_child,
    check_to_density,
    leaf_lists,
    leaf_ghosts,
    parent_lists,
    parent_ghosts,
):
    rows, columns = lax.axis_size("row"), lax.axis_size("col")
    column = lax.axis_index("col")
    planes = leaf_up.transpose(1, 0, 2)
    parent_up, parent_sent, zero = raise_parents(planes, parent_ghosts[0], child_to_parent)
    parent_came = lax.all_to_all(parent_sent, "col", split_axis=0, concat_axis=0, tiled=True)
    chosen = leaf_ghosts[0][message_order(column, columns)] + zero
    sent, direct = select_leaves(planes, chosen)
    came = lax.all_to_all(sent, "col", split_axis=0, concat_axis=0, tiled=True)
    ranks = range(rows * columns)
    half = [(d, d + NEAR if d % columns >= NEAR else d - NEAR) for d in ranks]
    direct = lax.ppermute(direct, ("row", "col"), [p for p in half if p[1] in ranks])
    parent_down = parent_level(
        parent_up,
        parent_came,
        order_lists(parent_lists, 64, 4, 8),
        translations,
        check_to_density,
        64,
        4,
        8,
    )
    lists = order_lists(leaf_lists, 256, 4, 4)
    came, parent_down, lists = lax.optimization_barrier((came, parent_down, lists))
    turn = [(d, d + columns if d % columns < NEAR else d - columns) for d in ranks]
    passing = lax.dynamic_slice_in_dim(came, jnp.where(column < NEAR, NEAR + 1, 0), NEAR - 1)
    shifted = lax.ppermute(passing, ("row", "col"), [p for p in turn if p[1] in ranks])
    leaf_down = leaf_level(
        planes,
        came,
        shifted,
        direct,
        message_origin(column, columns),
        parent_down,
        lists,
        translations,
        parent_to_child,
        check_to_density,
        256,
        4,
        4,
    )
    return leaf_down.transpose(1, 0, 2)


def solution(mesh):
    return jax.shard_map(
        local,
        mesh=mesh,
        in_specs=(
            P(("row", "col"), None, None),
            P(),
            P(),
            P(),
            P(),
            P(("row", "col"), None),
            P(("row", "col"), None, None),
            P(("row", "col"), None),
            P(("row", "col"), None, None),
        ),
        out_specs=P(("row", "col"), None, None),
        check_vma=False,
    )
```

time: 267 us -> 193 us (0.72)
  Pallas kernels: 179 us -> 123 us
  starting transfers between devices: 72.1 us -> 20.5 us
  waiting for transfers between devices: 5.61 us -> 30.5 us
  local copies, waits for them, and re-layouts: 5.37 us -> 12.3 us
    ppermute x16 -> x2, starting transfers between devices: 66.6 us -> 7.5 us  [the longest x1 5.4 us: local(): lax.ppermute(passing, ('row', 'col'), [p for p in turn if p[1] in ranks])]
    pallas_call x3 -> x4, Pallas kernels: 179 us -> 123 us  [the longest x1 97.5 us: leaf_level(): pl.pallas_call(kernel, in_specs=[smem, vmem, vmem, vmem, vmem, hbm, hbm,...]
    all_to_all x0 -> x1, waiting for transfers between devices: none -> 16.6 us  [local(): came = lax.all_to_all(sent, 'col', split_axis=0, concat_axis=0, tiled=True)]
    ppermute x16 -> x2, waiting for transfers between devices: 5.6 us -> 12.5 us  [the longest x1 7 us: local(): lax.ppermute(direct, ('row', 'col'), [p for p in half if p[1] in ranks])]
    all_to_all x0 -> x1, starting transfers between devices: none -> 5.23 us  [local(): came = lax.all_to_all(sent, 'col', split_axis=0, concat_axis=0, tiled=True)]
    reshape x0 -> x2, local copies, waits for them, and re-layouts: none -> 3.52 us  [order_lists(): return places.reshape(-1, 1, chunk_steps * group * block)]
  transfers between devices with their start and end apart: 17 -> 4, of which waited for: 1 -> 4; matrix products, arithmetic and copies ran while one was open for 2% -> 7% of each run, Pallas kernels for 10% -> 12%
where the time goes in v2:
time: 193 us; the launch traced here: 192 us
  Pallas kernels  123 us (64%)
  waiting for transfers between devices  30.5 us (16%)
  starting transfers between devices  20.5 us (11%)
  local copies, waits for them, and re-layouts  12.3 us (6%)
  other arithmetic  4.95 us (3%)
    pallas_call x1, Pallas kernels, leaf_level(): pl.pallas_call(kernel, in_specs=[smem, vmem, vmem, vmem, vmem, hbm, hbm,...  97.5 us
    pallas_call x1, Pallas kernels, parent_level(): pl.pallas_call(kernel, in_specs=[vmem, vmem, hbm, hbm, vmem], out_specs=v...  17.1 us
    all_to_all x1, waiting for transfers between devices, local(): came = lax.all_to_all(sent, 'col', split_axis=0, concat_axis=0, tiled=True)  16.6 us
    all_to_all x1, starting transfers between devices, local(): lax.all_to_all(parent_sent, 'col', split_axis=0, concat_axis=0, tiled=True)  7.79 us
    ppermute x1, waiting for transfers between devices, local(): lax.ppermute(direct, ('row', 'col'), [p for p in half if p[1] in ranks])  7 us
    pallas_call x1, Pallas kernels, select_leaves(): pl.pallas_call(kernel, in_specs=[vmem, pl.BlockSpec(memory_space=pltpu.SM...  5.8 us
    ppermute x1, waiting for transfers between devices, local(): lax.ppermute(passing, ('row', 'col'), [p for p in turn if p[1] in ranks])  5.5 us
    ppermute x1, starting transfers between devices, local(): lax.ppermute(passing, ('row', 'col'), [p for p in turn if p[1] in ranks])  5.4 us
  transfers between devices with their start and end apart: 4, of which 4 were waited for; matrix products, arithmetic and copies ran while one was open for 7% of the time, Pallas kernels for 12%

profile of v2, /device:TPU:3, one launch (start us, length us, event | category | flops | bytes accessed | tf_op | source)
XLA Modules:
  0.0 191.8 jit_solution(5068726105303781636)
XLA Ops:
  0.0 0.0 copy-start
  0.0 0.7 broadcast_multiply_fusion
  0.7 0.7 mul.46.ghosts_ref
  1.4 2.8 %raise_parents.1 = (bf16[3,64,128]{2,1,0:T(8,128)(2,1)}, bf16[16,3,32,128]{3,2,1,0:T(8,128)(2,1)}, s32[1,1]{1,0:T(1,128)}) custom-call(bf16[3,512,128]{2,1,0:T(8,128)(2,1)} %bitcast.23, s32[1,512]{1,0:T(1,128)} %mul.46.ghosts_ref, bf16[8,128,128]{2,1,0:T(8,128)(2,1)} %operators_ref.1), custom_call_target="tpu_custom_call" | custom-call | tf_op jit(solution)/shard_map/raise_parents/pallas_call | solution.py:63
  4.2 7.8 %all-to-all-start.1 = ((bf16[16,3,32,128]{3,2,1,0:T(8,128)(2,1)}), bf16[16,3,32,128]{3,2,1,0:T(8,128)(2,1)S(1)}, u32[]{:S(2)}, u32[]{:S(2)}) async-start(bf16[16,3,32,128]{3,2,1,0:T(8,128)(2,1)} %get-tuple-element.16), calls=%async_computation.1 | async-start | bytes 786432 | tf_op jit(solution)/shard_map/all_to_all | solution.py:359
  12.0 0.1 fusion.3
  12.1 0.0 copy-done
  12.1 0.6 gather_fusion
  12.7 0.6 multiply_bitcast_fusion.2
  13.3 0.6 copy.13
  14.0 5.8 %select_leaves.1 = (bf16[16,3,256,128]{3,2,1,0:T(8,128)(2,1)}, bf16[3,256,128]{2,1,0:T(8,128)(2,1)}) custom-call(bf16[3,512,128]{2,1,0:T(8,128)(2,1)} %bitcast.24, s32[1,4352]{1,0:T(1,128)} %bitcast.30), custom_call_target="tpu_custom_call" | custom-call | tf_op jit(solution)/shard_map/select_leaves/pallas_call | solution.py:93
  19.8 1.4 all-to-all-done.1.came_ref
  21.2 0.0 copy-start.2
  21.2 0.7 copy-done.2
  21.9 5.2 %all-to-all-start = ((bf16[16,3,256,128]{3,2,1,0:T(8,128)(2,1)}), bf16[16,3,256,128]{3,2,1,0:T(8,128)(2,1)S(1)}, u32[]{:S(2)}, u32[]{:S(2)}) async-start(bf16[16,3,256,128]{3,2,1,0:T(8,128)(2,1)} %get-tuple-element.14), calls=%async_computation | async-start | bytes 6291456 | tf_op jit(solution)/shard_map/all_to_all | solution.py:362
  27.2 0.9 multiply_bitcast_fusion.1
  28.1 0.1 copy.11
  28.2 0.1 reshape_transpose_reshape.3
  28.3 0.8 reshape.177.lists_hbm
  29.1 2.0 %multiply_bitcast_fusion = s32[316,512]{1,0:T(8,128)} fusion(s32[512,316]{0,1:T(8,128)} %param.14), kind=kLoop, calls=%fused_computation.1 | loop fusion | flops 323584 | bytes 1294336 | tf_op jit(solution)/shard_map/transpose | solution.py:113
  31.1 2.3 %reshape.178 = s32[79,4,2,256]{3,2,1,0:T(2,128)} reshape(s32[316,512]{1,0:T(8,128)} %multiply_bitcast_fusion) | data formatting | bytes 1294336 | tf_op jit(solution)/shard_map/reshape | solution.py:113
  33.4 1.3 copy.12
  34.6 0.1 pad.7
  34.8 0.1 copy.14
  34.9 0.9 concatenate.36
  35.8 2.8 %reshape.180.lists_hbm = s32[42,1,4096]{2,1,0:T(1,128)} reshape(s32[168,1024]{1,0:T(8,128)} %concatenate.36) | data formatting | bytes 1376256 | tf_op jit(solution)/shard_map/reshape | solution.py:119
  38.6 0.0 copy-start.5
  38.6 17.1 %parent_level.1.parent_ref = bf16[3,64,128]{2,1,0:T(8,128)(2,1)} custom-call(bf16[3,64,128]{2,1,0:T(8,128)(2,1)} %get-tuple-element.15.own_ref, bf16[16,3,32,128]{3,2,1,0:T(8,128)(2,1)} %copy-done.2, s32[12,1,2048]{2,1,0:T(1,128)} %reshape.177.lists_hbm, bf16[316,128,128]{2,1,0:T(8,128)(2,1)} %operators_hbm.3, bf16[128,128]{1,0:T(8,128)(2,1)} %inverse_ref.3), custom_call_target="tpu_custom_call" | custom-call | tf_op jit(solution)/shard_map/parent_level/pallas_call | solution.py:216
  55.6 16.6 %all-to-all-done.came_hbm = bf16[16,3,256,128]{3,2,1,0:T(8,128)(2,1)S(1)} async-done(((bf16[16,3,256,128]{3,2,1,0:T(8,128)(2,1)}), bf16[16,3,256,128]{3,2,1,0:T(8,128)(2,1)S(1)}, u32[]{:S(2)}, u32[]{:S(2)}) %all-to-all-start) | async-done | bytes 3145760 | tf_op jit(solution)/shard_map/all_to_all | solution.py:362
  72.2 0.0 copy-start.1
  72.2 0.1 constant_dynamic-slice_fusion
  72.3 5.4 %collective-permute-start = (bf16[7,3,256,128]{3,2,1,0:T(8,128)(2,1)S(1)}, bf16[7,3,256,128]{3,2,1,0:T(8,128)(2,1)S(1)}, u32[]{:S(2)}, u32[]{:S(2)}) collective-permute-start(bf16[7,3,256,128]{3,2,1,0:T(8,128)(2,1)S(1)} %constant_dynamic-slice_fusion), channel_id=1, source_target_pairs={{0,16},{1,17},{2,18},{3,19},{4,20},{5,21},{6,22},{7,23},{16,32},{1... | collective-permute-start | bytes 4128776 | tf_op jit(solution)/shard_map/ppermute | solution.py:380
  77.8 0.0 copy-done.5
  77.8 2.1 %collective-permute-start.1 = (bf16[3,256,128]{2,1,0:T(8,128)(2,1)S(1)}, bf16[3,256,128]{2,1,0:T(8,128)(2,1)S(1)}, u32[]{:S(2)}, u32[]{:S(2)}) collective-permute-start(bf16[3,256,128]{2,1,0:T(8,128)(2,1)S(1)} %copy-done.5), channel_id=1, source_target_pairs={{8,16},{9,17},{10,18},{11,19},{12,20},{13,21},{14,22},{15,23},{16,... | collective-permute-start | bytes 589832 | tf_op jit(solution)/shard_map/ppermute | solution.py:365
  79.9 0.6 pad_add_fusion.origin_ref
  80.5 7.0 %collective-permute-done.1.direct_hbm = bf16[3,256,128]{2,1,0:T(8,128)(2,1)S(1)} collective-permute-done((bf16[3,256,128]{2,1,0:T(8,128)(2,1)S(1)}, bf16[3,256,128]{2,1,0:T(8,128)(2,1)S(1)}, u32[]{:S(2)}, u32[]{:S(2)}) %collective-permute-start.1) | collective-permute-done | bytes 196640 | tf_op jit(solution)/shard_map/ppermute | solution.py:365
  87.5 0.0 copy-start.4
  87.5 5.5 %collective-permute-done.shifted_hbm = bf16[7,3,256,128]{3,2,1,0:T(8,128)(2,1)S(1)} collective-permute-done((bf16[7,3,256,128]{3,2,1,0:T(8,128)(2,1)S(1)}, bf16[7,3,256,128]{3,2,1,0:T(8,128)(2,1)S(1)}, u32[]{:S(2)}, u32[]{:S(2)}) %collective-permute-start) | collective-permute-done | bytes 1376288 | tf_op jit(solution)/shard_map/ppermute | solution.py:380
  93.0 0.0 copy-done.1
  93.0 0.0 copy-done.4
  93.0 0.0 copy-start.3
  93.0 1.1 copy-done.3
  94.1 97.5 %leaf_level.1 = bf16[3,512,128]{2,1,0:T(8,128)(2,1)} custom-call(s32[2,16]{1,0:T(2,128)} %pad_add_fusion.origin_ref, bf16[3,512,128]{2,1,0:T(8,128)(2,1)} %bitcast.25, bf16[3,64,128]{2,1,0:T(8,128)(2,1)} %parent_level.1.parent_ref, bf16[8,128,128]{2,1,0:T(8,128)(2,1)} %to_child_ref.1, bf16[128,128]{1,0:T(8,128)(2,1)} %inverse_ref.3, ...), custom_call_target="tpu_custom_call" | custom-call | tf_op jit(solution)/shard_map/leaf_level/pallas_call | solution.py:296
  (4 shorter events, 0.0 us)
Async XLA Ops:
  0.0 12.1 %copy-start = (s32[1,16,256]{2,1,0:T(8,128)S(1)}, s32[1,16,256]{2,1,0:T(8,128)}, u32[]{:S(2)}) copy-start(s32[1,16,256]{2,1,0:T(8,128)} %param.15) | copy-start | bytes 49156
  4.2 17.0 %all-to-all-start.1 = ((bf16[16,3,32,128]{3,2,1,0:T(8,128)(2,1)}), bf16[16,3,32,128]{3,2,1,0:T(8,128)(2,1)S(1)}, u32[]{:S(2)}, u32[]{:S(2)}) async-start(bf16[16,3,32,128]{3,2,1,0:T(8,128)(2,1)} %get-tuple-element.16), calls=%async_computation.1 | async-start | bytes 786432 | tf_op jit(solution)/shard_map/all_to_all | solution.py:359
  21.2 0.7 copy-start.2
  21.9 50.3 %all-to-all-start = ((bf16[16,3,256,128]{3,2,1,0:T(8,128)(2,1)}), bf16[16,3,256,128]{3,2,1,0:T(8,128)(2,1)S(1)}, u32[]{:S(2)}, u32[]{:S(2)}) async-start(bf16[16,3,256,128]{3,2,1,0:T(8,128)(2,1)} %get-tuple-element.14), calls=%async_computation | async-start | bytes 6291456 | tf_op jit(solution)/shard_map/all_to_all | solution.py:362
  38.6 39.2 %copy-start.5 = (bf16[3,256,128]{2,1,0:T(8,128)(2,1)S(1)}, bf16[3,256,128]{2,1,0:T(8,128)(2,1)}, u32[]{:S(2)}) copy-start(bf16[3,256,128]{2,1,0:T(8,128)(2,1)} %get-tuple-element.20) | copy-start | bytes 589828
  72.2 20.8 %copy-start.1 = (bf16[16,3,256,128]{3,2,1,0:T(8,128)(2,1)}, bf16[16,3,256,128]{3,2,1,0:T(8,128)(2,1)S(1)}, u32[]{:S(2)}) copy-start(bf16[16,3,256,128]{3,2,1,0:T(8,128)(2,1)S(1)} %all-to-all-done.came_hbm) | copy-start | bytes 9437188
  72.3 20.6 %collective-permute-start = (bf16[7,3,256,128]{3,2,1,0:T(8,128)(2,1)S(1)}, bf16[7,3,256,128]{3,2,1,0:T(8,128)(2,1)S(1)}, u32[]{:S(2)}, u32[]{:S(2)}) collective-permute-start(bf16[7,3,256,128]{3,2,1,0:T(8,128)(2,1)S(1)} %constant_dynamic-slice_fusion), channel_id=1, source_target_pairs={{0,16},{1,17},{2,18},{3,19},{4,20},{5,21},{6,22},{7,23},{16,32},{1... | collective-permute-start | bytes 4128776 | tf_op jit(solution)/shard_map/ppermute | solution.py:380
  77.8 9.7 %collective-permute-start.1 = (bf16[3,256,128]{2,1,0:T(8,128)(2,1)S(1)}, bf16[3,256,128]{2,1,0:T(8,128)(2,1)S(1)}, u32[]{:S(2)}, u32[]{:S(2)}) collective-permute-start(bf16[3,256,128]{2,1,0:T(8,128)(2,1)S(1)} %copy-done.5), channel_id=1, source_target_pairs={{8,16},{9,17},{10,18},{11,19},{12,20},{13,21},{14,22},{15,23},{16,... | collective-permute-start | bytes 589832 | tf_op jit(solution)/shard_map/ppermute | solution.py:365
  87.5 5.5 %copy-start.4 = (bf16[3,256,128]{2,1,0:T(8,128)(2,1)}, bf16[3,256,128]{2,1,0:T(8,128)(2,1)S(1)}, u32[]{:S(2)}) copy-start(bf16[3,256,128]{2,1,0:T(8,128)(2,1)S(1)} %collective-permute-done.1.direct_hbm) | copy-start | bytes 589828
  93.0 1.1 copy-start.3

commit v3 on v2

--- a/solution.py
+++ b/solution.py
@@ -39,72 +39,60 @@
         out_ref[k] = gathered[pl.ds(k, count, stride=4), :].astype(jnp.bfloat16)
 
 
-def raise_parents(planes, ghosts, operators):
+def prepare(planes, ghosts, parent_ghosts, operators):
     boxes = planes.shape[1]
     parents = boxes // 8
-    columns, slots = ghosts.shape
+    messages, slots = ghosts.shape
+    columns, parent_slots = parent_ghosts.shape
+    passed = messages - columns - 1
 
     def kernel(
-        planes_ref, ghosts_ref, operators_ref, up_ref, sent_ref, zero_ref, table, own, gathered
+        planes_ref, ghosts_ref, parent_ghosts_ref, operators_ref,
+        sent_ref, passing_ref, direct_ref, up_ref, parent_sent_ref,
+        table, own, gathered, parent_gathered,
     ):
-        zero_ref[0, 0] = 0
-        spread(table, 0, planes_ref)
+        spread(table, 4, planes_ref)
         matrices = jnp.concatenate([operators_ref[c] for c in range(8)], axis=1)
         for k in range(3):
             children = jnp.concatenate(
-                [table[pl.ds(4 * c + k, parents, stride=32), :] for c in range(8)], axis=1
+                [table[pl.ds(4 + 4 * c + k, parents, stride=32), :] for c in range(8)], axis=1
             )
             up_ref[k] = dot_nt(children.astype(jnp.bfloat16), matrices).astype(jnp.bfloat16)
         spread(own, 4, up_ref)
         for column in range(columns):
-            select_rows(own, ghosts_ref, column * slots, slots, gathered, sent_ref.at[column])
+            select_rows(
+                own, parent_ghosts_ref, column * parent_slots, parent_slots, parent_gathered,
+                parent_sent_ref.at[column],
+            )
+        targets = [sent_ref.at[i] for i in range(columns)]
+        targets += [passing_ref.at[i] for i in range(passed)] + [direct_ref]
+        for which, target in enumerate(targets):
+            select_rows(table, ghosts_ref, which * slots, slots, gathered, target)
 
     vmem = pl.BlockSpec(memory_space=pltpu.VMEM)
+    smem = pl.BlockSpec(memory_space=pltpu.SMEM)
     return pl.pallas_call(
         kernel,
-        in_specs=[vmem, pl.BlockSpec(memory_space=pltpu.SMEM), vmem],
-        out_specs=[vmem, vmem, pl.BlockSpec(memory_space=pltpu.SMEM)],
+        in_specs=[vmem, smem, smem, vmem],
+        out_specs=[vmem] * 5,
         out_shape=[
+            jax.ShapeDtypeStruct((columns, 3, slots, 128), jnp.bfloat16),
+            jax.ShapeDtypeStruct((passed, 3, slots, 128), jnp.bfloat16),
+            jax.ShapeDtypeStruct((3, slots, 128), jnp.bfloat16),
             jax.ShapeDtypeStruct((3, parents, 128), jnp.bfloat16),
-            jax.ShapeDtypeStruct((columns, 3, slots, 128), jnp.bfloat16),
-            jax.ShapeDtypeStruct((1, 1), jnp.int32),
-        ],
-        scratch_shapes=[
-            pltpu.VMEM((4 * boxes, 128), jnp.float32),
-            pltpu.VMEM((4 * parents + 16, 128), jnp.float32),
-            pltpu.VMEM((4 * slots, 128), jnp.float32),
-        ],
-        compiler_params=pltpu.CompilerParams(vmem_limit_bytes=VMEM_BYTES),
-        name="raise_parents",
-    )(planes, (ghosts * 4).reshape(1, -1), operators)
-
-
-def select_leaves(planes, ghosts):
-    boxes = planes.shape[1]
-    messages, slots = ghosts.shape
-
-    def kernel(planes_ref, ghosts_ref, sent_ref, direct_ref, table, gathered):
-        spread(table, 4, planes_ref)
-        for which in range(messages):
-            target = direct_ref if which == messages - 1 else sent_ref.at[which]
-            select_rows(table, ghosts_ref, which * slots, slots, gathered, target)
-
-    vmem = pl.BlockSpec(memory_space=pltpu.VMEM)
-    return pl.pallas_call(
-        kernel,
-        in_specs=[vmem, pl.BlockSpec(memory_space=pltpu.SMEM)],
-        out_specs=[vmem, vmem],
-        out_shape=[
-            jax.ShapeDtypeStruct((messages - 1, 3, slots, 128), jnp.bfloat16),
-            jax.ShapeDtypeStruct((3, slots, 128), jnp.bfloat16),
+            jax.ShapeDtypeStruct((columns, 3, parent_slots, 128), jnp.bfloat16),
         ],
         scratch_shapes=[
             pltpu.VMEM((4 * boxes + 16, 128), jnp.float32),
+            pltpu.VMEM((4 * parents + 16, 128), jnp.float32),
             pltpu.VMEM((4 * slots, 128), jnp.float32),
+            pltpu.VMEM((4 * parent_slots, 128), jnp.float32),
         ],
         compiler_params=pltpu.CompilerParams(vmem_limit_bytes=VMEM_BYTES),
-        name="select_leaves",
-    )(planes, (ghosts * 4).reshape(1, -1))
+        name="prepare",
+    )(
+        planes, (ghosts * 4).reshape(1, -1), (parent_ghosts * 4).reshape(1, -1), operators
+    )
 
 
 def order_lists(lists, block, group, chunk_steps):
@@ -233,7 +221,7 @@
 
 
 def leaf_level(
-    own, came, shifted, direct, origin, parent_down, lists, translations, to_child, inverse,
+    own, came, direct, origin, parent_down, lists, translations, to_child, inverse,
     block, group, chunk_steps,
 ):
     boxes = own.shape[1]
@@ -245,7 +233,7 @@
 
     def kernel(
         origin_ref, own_ref, parent_ref, to_child_ref, inverse_ref, lists_hbm, operators_hbm,
-        came_hbm, shifted_hbm, direct_hbm, out_ref,
+        came_hbm, direct_hbm, out_ref,
         table, operators, ghosts, total, result, chunk, chunk_sem, operator_sem, ghost_sem,
     ):
         def ghost_copy(source, j):
@@ -254,8 +242,7 @@
         for j in range(offsets):
             kind, place = origin_ref[0, j], origin_ref[1, j]
             pl.when(kind == 0)(lambda: ghost_copy(came_hbm.at[place], j).start())
-            pl.when(kind == 1)(lambda: ghost_copy(shifted_hbm.at[place], j).start())
-            pl.when(kind == 2)(lambda: ghost_copy(direct_hbm, j).start())
+            pl.when(kind == 1)(lambda: ghost_copy(direct_hbm, j).start())
         first_fetches(lists_hbm, chunk, chunk_sem)
         early, late = split_operator_copy(operators_hbm, operators, operator_sem, first)
         early.start()
@@ -295,7 +282,7 @@
     hbm = pl.BlockSpec(memory_space=pl.ANY)
     return pl.pallas_call(
         kernel,
-        in_specs=[smem, vmem, vmem, vmem, vmem, hbm, hbm, hbm, hbm, hbm],
+        in_specs=[smem, vmem, vmem, vmem, vmem, hbm, hbm, hbm, hbm],
         out_specs=vmem,
         out_shape=jax.ShapeDtypeStruct((3, boxes, 128), jnp.bfloat16),
         scratch_shapes=[
@@ -312,7 +299,7 @@
         compiler_params=pltpu.CompilerParams(vmem_limit_bytes=VMEM_BYTES),
         name="leaf_level",
     )(
-        origin, own, parent_down, to_child, inverse, lists, translations, came, shifted, direct
+        origin, own, parent_down, to_child, inverse, lists, translations, came, direct
     )
 
 
@@ -320,13 +307,14 @@
     return jnp.where(distance > 0, distance - 1, NEAR - 1 - distance)
 
 
-def message_order(column, columns):
+def message_order(column, columns, start):
     difference = jnp.arange(columns) - column
-    distance = jnp.where(difference > NEAR, difference - columns, difference)
-    distance = jnp.where(distance < -NEAR, distance + columns, distance)
-    order = jnp.where(distance == 0, 0, offset_index(distance))
+    order = jnp.where(jnp.abs(difference) > NEAR, 0, offset_index(difference))
+    beside = start + jnp.arange(NEAR - 1) - column
+    beside = jnp.where(column < NEAR, beside - columns, beside + columns)
+    beside = jnp.where(jnp.abs(beside) < NEAR, offset_index(beside), 0)
     last = offset_index(jnp.where(column < NEAR, -NEAR, NEAR))
-    return jnp.concatenate([order, last[None]])
+    return jnp.concatenate([jnp.where(difference == 0, 0, order), beside, last[None]])
 
 
 def message_origin(column, columns):
@@ -334,11 +322,8 @@
     distance = jnp.where(offset < NEAR, offset + 1, NEAR - 1 - offset)
     sender = column - distance
     inside = (sender >= 0) & (sender < columns)
-    direct = jnp.abs(distance) == NEAR
-    kind = jnp.where(inside, 0, jnp.where(direct, 2, 1))
-    turned = jnp.where(sender < 0, sender + NEAR - 1, sender - columns)
-    place = jnp.where(inside, sender, jnp.where(direct, 0, turned))
-    return jnp.stack([kind, place]).astype(jnp.int32)
+    kind = jnp.where(inside | (jnp.abs(distance) < NEAR), 0, 1)
+    return jnp.stack([kind, sender % columns]).astype(jnp.int32)
 
 
 def local(
@@ -355,14 +340,23 @@
     rows, columns = lax.axis_size("row"), lax.axis_size("col")
     column = lax.axis_index("col")
     planes = leaf_up.transpose(1, 0, 2)
-    parent_up, parent_sent, zero = raise_parents(planes, parent_ghosts[0], child_to_parent)
+    start = jnp.where(column < NEAR, NEAR + 1, 0)
+    chosen = leaf_ghosts[0][message_order(column, columns, start)]
+    sent, passing, direct, parent_up, parent_sent = prepare(
+        planes, chosen, parent_ghosts[0], child_to_parent
+    )
     parent_came = lax.all_to_all(parent_sent, "col", split_axis=0, concat_axis=0, tiled=True)
-    chosen = leaf_ghosts[0][message_order(column, columns)] + zero
-    sent, direct = select_leaves(planes, chosen)
-    came = lax.all_to_all(sent, "col", split_axis=0, concat_axis=0, tiled=True)
     ranks = range(rows * columns)
+    turn = [(d, d - columns if d % columns < NEAR else d + columns) for d in ranks]
+    shifted = lax.ppermute(passing, ("row", "col"), [p for p in turn if p[1] in ranks])
     half = [(d, d + NEAR if d % columns >= NEAR else d - NEAR) for d in ranks]
     direct = lax.ppermute(direct, ("row", "col"), [p for p in half if p[1] in ranks])
+    foreign = jnp.abs(start + jnp.arange(NEAR - 1) - column) > NEAR
+    kept = lax.dynamic_slice_in_dim(sent, start, NEAR - 1)
+    shifted = jnp.where(foreign[:, None, None, None], shifted, kept)
+    sent = lax.dynamic_update_slice_in_dim(sent, shifted, start, 0)
+    sent, direct, parent_came = lax.optimization_barrier((sent, direct, parent_came))
+    came = lax.all_to_all(sent, "col", split_axis=0, concat_axis=0, tiled=True)
     parent_down = parent_level(
         parent_up,
         parent_came,
@@ -375,13 +369,9 @@
     )
     lists = order_lists(leaf_lists, 256, 4, 4)
     came, parent_down, lists = lax.optimization_barrier((came, parent_down, lists))
-    turn = [(d, d + columns if d % columns < NEAR else d - columns) for d in ranks]
-    passing = lax.dynamic_slice_in_dim(came, jnp.where(column < NEAR, NEAR + 1, 0), NEAR - 1)
-    shifted = lax.ppermute(passing, ("row", "col"), [p for p in turn if p[1] in ranks])
     leaf_down = leaf_level(
         planes,
         came,
-        shifted,
         direct,
         message_origin(column, columns),
         parent_down,

time: 193 us -> 190 us (0.984); the launches traced: 192 us -> 187 us
  waiting for transfers between devices: 30.5 us -> 22.7 us
  other arithmetic: 4.95 us -> 7.21 us
    ppermute x1, waiting for transfers between devices: 7 us -> 0.01 us  [local(): lax.ppermute(direct, ('row', 'col'), [p for p in half if p[1] in ranks])]
    ppermute x1, starting transfers between devices: 2.1 us -> 5.39 us  [local(): lax.ppermute(direct, ('row', 'col'), [p for p in half if p[1] in ranks])]
    dynamic_update_slice x0 -> x1, other arithmetic: none -> 2.89 us  [local(): sent = lax.dynamic_update_slice_in_dim(sent, shifted, start, 0)]
    ppermute x1, starting transfers between devices: 5.4 us -> 2.58 us  [local(): lax.ppermute(passing, ('row', 'col'), [p for p in turn if p[1] in ranks])]
    all_to_all x1, starting transfers between devices: 7.79 us -> 5.4 us  [local(): lax.all_to_all(parent_sent, 'col', split_axis=0, concat_axis=0, tiled=True)]
    unnamed x15 -> x11, local copies, waits for them, and re-layouts: 2.69 us -> 3.87 us
    pallas_call x2 -> x1, Pallas kernels: 8.63 us -> 8.15 us  [prepare(): pl.pallas_call(kernel, in_specs=[vmem, smem, smem, vmem], out_specs=[vmem...]
  transfers between devices with their start and end apart: 4 -> 4, of which waited for: 4 -> 2; matrix products, arithmetic and copies ran while one was open for 7% -> 8% of each run, Pallas kernels for 12% -> 9%
where the time goes in v3:
time: 190 us; the launch traced here: 187 us
  Pallas kernels  123 us (65%)
  waiting for transfers between devices  22.7 us (12%)
  starting transfers between devices  20.2 us (11%)
  local copies, waits for them, and re-layouts  13.3 us (7%)
  other arithmetic  7.21 us (4%)
    pallas_call x1, Pallas kernels, leaf_level(): pl.pallas_call(kernel, in_specs=[smem, vmem, vmem, vmem, vmem, hbm, hbm,...  97.7 us
    pallas_call x1, Pallas kernels, parent_level(): pl.pallas_call(kernel, in_specs=[vmem, vmem, hbm, hbm, vmem], out_specs=v...  17 us
    all_to_all x1, waiting for transfers between devices, local(): came = lax.all_to_all(sent, 'col', split_axis=0, concat_axis=0, tiled=True)  15.9 us
    pallas_call x1, Pallas kernels, prepare(): pl.pallas_call(kernel, in_specs=[vmem, smem, smem, vmem], out_specs=[vmem...  8.15 us
    all_to_all x1, starting transfers between devices, local(): came = lax.all_to_all(sent, 'col', split_axis=0, concat_axis=0, tiled=True)  6.84 us
    ppermute x1, waiting for transfers between devices, local(): lax.ppermute(passing, ('row', 'col'), [p for p in turn if p[1] in ranks])  6.75 us
    all_to_all x1, starting transfers between devices, local(): lax.all_to_all(parent_sent, 'col', split_axis=0, concat_axis=0, tiled=True)  5.4 us
    ppermute x1, starting transfers between devices, local(): lax.ppermute(direct, ('row', 'col'), [p for p in half if p[1] in ranks])  5.39 us
  transfers between devices with their start and end apart: 4, of which 2 were waited for; matrix products, arithmetic and copies ran while one was open for 8% of the time, Pallas kernels for 9%

profile of v3, /device:TPU:3, one launch (start us, length us, event | category | flops | bytes accessed | tf_op | source)
XLA Modules:
  0.0 186.5 jit_solution(17998703901300211744)
XLA Ops:
  0.0 0.0 copy-start
  0.0 0.1 fusion.3
  0.1 0.6 copy-done
  0.7 0.6 gather_fusion
  1.3 0.6 copy.13
  1.9 0.7 broadcast_multiply_fusion
  2.6 0.6 mul.49.parent_ghosts_ref
  3.3 8.2 %prepare.1 = (bf16[16,3,256,128]{3,2,1,0:T(8,128)(2,1)}, bf16[7,3,256,128]{3,2,1,0:T(8,128)(2,1)}, bf16[3,256,128]{2,1,0:T(8,128)(2,1)}, bf16[3,64,128]{2,1,0:T(8,128)(2,1)}, bf16[16,3,32,128]{3,2,1,0:T(8,128)(2,1)}) custom-call(bf16[3,512,128]{2,1,0:T(8,128)(2,1)} %bitcast.28, s32[1,6144]{1,0:T(1,128)} %bitcast.30, s32[1,512]{1,0:T(1,128)} %mul.49.parent_ghosts_ref, ...), custom_call_target="tpu_custom_call" | custom-call | tf_op jit(solution)/shard_map/prepare/pallas_call | solution.py:74
  11.4 2.6 %collective-permute-start = (bf16[7,3,256,128]{3,2,1,0:T(8,128)(2,1)}, bf16[7,3,256,128]{3,2,1,0:T(8,128)(2,1)S(1)}, u32[]{:S(2)}, u32[]{:S(2)}) collective-permute-start(bf16[7,3,256,128]{3,2,1,0:T(8,128)(2,1)} %get-tuple-element.17), channel_id=1, source_target_pairs={{8,24},{9,25},{10,26},{11,27},{12,28},{13,29},{14,30},{15,31},{16,... | collective-permute-start | bytes 4128776 | tf_op jit(solution)/shard_map/ppermute | solution.py:351
  14.0 5.4 %collective-permute-start.1 = (bf16[3,256,128]{2,1,0:T(8,128)(2,1)}, bf16[3,256,128]{2,1,0:T(8,128)(2,1)S(1)}, u32[]{:S(2)}, u32[]{:S(2)}) collective-permute-start(bf16[3,256,128]{2,1,0:T(8,128)(2,1)} %get-tuple-element.18), channel_id=1, source_target_pairs={{8,16},{9,17},{10,18},{11,19},{12,20},{13,21},{14,22},{15,23},{16,... | collective-permute-start | bytes 589832 | tf_op jit(solution)/shard_map/ppermute | solution.py:353
  19.4 5.4 %all-to-all-start = ((bf16[16,3,32,128]{3,2,1,0:T(8,128)(2,1)}), bf16[16,3,32,128]{3,2,1,0:T(8,128)(2,1)S(1)}, u32[]{:S(2)}, u32[]{:S(2)}) async-start(bf16[16,3,32,128]{3,2,1,0:T(8,128)(2,1)} %get-tuple-element.19), calls=%async_computation | async-start | bytes 786432 | tf_op jit(solution)/shard_map/all_to_all | solution.py:348
  24.8 6.8 %collective-permute-done = bf16[7,3,256,128]{3,2,1,0:T(8,128)(2,1)S(1)} collective-permute-done((bf16[7,3,256,128]{3,2,1,0:T(8,128)(2,1)}, bf16[7,3,256,128]{3,2,1,0:T(8,128)(2,1)S(1)}, u32[]{:S(2)}, u32[]{:S(2)}) %collective-permute-start) | collective-permute-done | bytes 1376288 | tf_op jit(solution)/shard_map/ppermute | solution.py:351
  31.6 2.9 %select_dynamic-update-slice_fusion = bf16[16,3,256,128]{3,2,1,0:T(8,128)(2,1)} fusion(bf16[16,3,256,128]{3,2,1,0:T(8,128)(2,1)} %get-tuple-element.16, s32[]{:T(128)S(6)} %select_n.174, bf16[7,3,256,128]{3,2,1,0:T(8,128)(2,1)S(1)} %collective-permute-done, pred[7]{0:T(512)(128)(4,1)S(1)} %abs_compare_fusion), kind=kLoop, calls=%fused_computation.1 | loop fusion | flops 688128 | bytes 4128779 | tf_op jit(solution)/shard_map/dynamic_update_slice | solution.py:357
  34.5 0.0 collective-permute-done.1.direct_hbm
  34.5 0.0 copy-start.3
  34.5 0.0 all-to-all-done.came_ref
  34.5 0.0 copy-start.2
  34.5 0.7 copy-done.3
  35.2 0.1 copy-done.2
  35.3 6.8 %all-to-all-start.1 = ((bf16[16,3,256,128]{3,2,1,0:T(8,128)(2,1)}), bf16[16,3,256,128]{3,2,1,0:T(8,128)(2,1)S(1)}, u32[]{:S(2)}, u32[]{:S(2)}) async-start(bf16[16,3,256,128]{3,2,1,0:T(8,128)(2,1)} %select_dynamic-update-slice_fusion), calls=%async_computation.1 | async-start | bytes 6291456 | tf_op jit(solution)/shard_map/all_to_all | solution.py:359
  42.1 0.9 multiply_bitcast_fusion.1
  43.0 0.1 copy.11
  43.2 0.1 reshape_transpose_reshape.3
  43.3 0.7 reshape.216.lists_hbm
  44.0 2.0 %multiply_bitcast_fusion = s32[316,512]{1,0:T(8,128)} fusion(s32[512,316]{0,1:T(8,128)} %param.14), kind=kLoop, calls=%fused_computation.2 | loop fusion | flops 323584 | bytes 1294336 | tf_op jit(solution)/shard_map/transpose | solution.py:101
  46.0 2.3 %reshape.217 = s32[79,4,2,256]{3,2,1,0:T(2,128)} reshape(s32[316,512]{1,0:T(8,128)} %multiply_bitcast_fusion) | data formatting | bytes 1294336 | tf_op jit(solution)/shard_map/reshape | solution.py:101
  48.3 1.3 copy.12
  49.6 0.1 pad.8
  49.7 0.1 copy.14
  49.8 0.9 concatenate.39
  50.7 2.8 %reshape.219.lists_hbm = s32[42,1,4096]{2,1,0:T(1,128)} reshape(s32[168,1024]{1,0:T(8,128)} %concatenate.39) | data formatting | bytes 1376256 | tf_op jit(solution)/shard_map/reshape | solution.py:107
  53.5 0.6 pad_add_fusion.origin_ref
  54.1 17.0 %parent_level.1.parent_ref = bf16[3,64,128]{2,1,0:T(8,128)(2,1)} custom-call(bf16[3,64,128]{2,1,0:T(8,128)(2,1)} %get-tuple-element.21.own_ref, bf16[16,3,32,128]{3,2,1,0:T(8,128)(2,1)} %copy-done.2, s32[12,1,2048]{2,1,0:T(1,128)} %reshape.216.lists_hbm, bf16[316,128,128]{2,1,0:T(8,128)(2,1)} %operators_hbm.3, bf16[128,128]{1,0:T(8,128)(2,1)} %inverse_ref.3), custom_call_target="tpu_custom_call" | custom-call | tf_op jit(solution)/shard_map/parent_level/pallas_call | solution.py:204
  71.1 15.9 %all-to-all-done.1.came_hbm = bf16[16,3,256,128]{3,2,1,0:T(8,128)(2,1)S(1)} async-done(((bf16[16,3,256,128]{3,2,1,0:T(8,128)(2,1)}), bf16[16,3,256,128]{3,2,1,0:T(8,128)(2,1)S(1)}, u32[]{:S(2)}, u32[]{:S(2)}) %all-to-all-start.1) | async-done | bytes 3145760 | tf_op jit(solution)/shard_map/all_to_all | solution.py:359
  87.0 0.0 copy-start.1
  87.0 1.6 copy-done.1
  88.7 97.7 %leaf_level.1 = bf16[3,512,128]{2,1,0:T(8,128)(2,1)} custom-call(s32[2,16]{1,0:T(2,128)} %pad_add_fusion.origin_ref, bf16[3,512,128]{2,1,0:T(8,128)(2,1)} %bitcast.29, bf16[3,64,128]{2,1,0:T(8,128)(2,1)} %parent_level.1.parent_ref, bf16[8,128,128]{2,1,0:T(8,128)(2,1)} %to_child_ref.1, bf16[128,128]{1,0:T(8,128)(2,1)} %inverse_ref.3, ...), custom_call_target="tpu_custom_call" | custom-call | tf_op jit(solution)/shard_map/leaf_level/pallas_call | solution.py:283
  (7 shorter events, 0.1 us)
Async XLA Ops:
  0.0 0.7 copy-start
  11.4 20.2 %collective-permute-start = (bf16[7,3,256,128]{3,2,1,0:T(8,128)(2,1)}, bf16[7,3,256,128]{3,2,1,0:T(8,128)(2,1)S(1)}, u32[]{:S(2)}, u32[]{:S(2)}) collective-permute-start(bf16[7,3,256,128]{3,2,1,0:T(8,128)(2,1)} %get-tuple-element.17), channel_id=1, source_target_pairs={{8,24},{9,25},{10,26},{11,27},{12,28},{13,29},{14,30},{15,31},{16,... | collective-permute-start | bytes 4128776 | tf_op jit(solution)/shard_map/ppermute | solution.py:351
  14.0 20.5 %collective-permute-start.1 = (bf16[3,256,128]{2,1,0:T(8,128)(2,1)}, bf16[3,256,128]{2,1,0:T(8,128)(2,1)S(1)}, u32[]{:S(2)}, u32[]{:S(2)}) collective-permute-start(bf16[3,256,128]{2,1,0:T(8,128)(2,1)} %get-tuple-element.18), channel_id=1, source_target_pairs={{8,16},{9,17},{10,18},{11,19},{12,20},{13,21},{14,22},{15,23},{16,... | collective-permute-start | bytes 589832 | tf_op jit(solution)/shard_map/ppermute | solution.py:353
  19.4 15.1 %all-to-all-start = ((bf16[16,3,32,128]{3,2,1,0:T(8,128)(2,1)}), bf16[16,3,32,128]{3,2,1,0:T(8,128)(2,1)S(1)}, u32[]{:S(2)}, u32[]{:S(2)}) async-start(bf16[16,3,32,128]{3,2,1,0:T(8,128)(2,1)} %get-tuple-element.19), calls=%async_computation | async-start | bytes 786432 | tf_op jit(solution)/shard_map/all_to_all | solution.py:348
  34.5 0.7 copy-start.3
  34.5 0.8 copy-start.2
  35.3 51.7 %all-to-all-start.1 = ((bf16[16,3,256,128]{3,2,1,0:T(8,128)(2,1)}), bf16[16,3,256,128]{3,2,1,0:T(8,128)(2,1)S(1)}, u32[]{:S(2)}, u32[]{:S(2)}) async-start(bf16[16,3,256,128]{3,2,1,0:T(8,128)(2,1)} %select_dynamic-update-slice_fusion), calls=%async_computation.1 | async-start | bytes 6291456 | tf_op jit(solution)/shard_map/all_to_all | solution.py:359
  87.0 1.6 copy-start.1

commit v4 on v3

--- a/solution.py
+++ b/solution.py
@@ -28,12 +28,12 @@
         table[pl.ds(at + k, plane.shape[0], stride=4), :] = plane.astype(jnp.float32)
 
 
-def select_rows(table, places_ref, start, count, gathered, out_ref):
+def select_rows(table, places_ref, start, count, scale, gathered, out_ref):
     low_half = lax.broadcasted_iota(jnp.int32, (8, 128), 0) < 4
     for pair in range(count // 2):
         at = start + 2 * pair
         gathered[8 * pair : 8 * pair + 8, :] = pick_pair(
-            table, low_half, places_ref[0, at], places_ref[0, at + 1]
+            table, low_half, scale * places_ref[0, at], scale * places_ref[0, at + 1]
         )
     for k in range(3):
         out_ref[k] = gathered[pl.ds(k, count, stride=4), :].astype(jnp.bfloat16)
@@ -61,13 +61,13 @@
         spread(own, 4, up_ref)
         for column in range(columns):
             select_rows(
-                own, parent_ghosts_ref, column * parent_slots, parent_slots, parent_gathered,
+                own, parent_ghosts_ref, column * parent_slots, parent_slots, 4, parent_gathered,
                 parent_sent_ref.at[column],
             )
         targets = [sent_ref.at[i] for i in range(columns)]
         targets += [passing_ref.at[i] for i in range(passed)] + [direct_ref]
         for which, target in enumerate(targets):
-            select_rows(table, ghosts_ref, which * slots, slots, gathered, target)
+            select_rows(table, ghosts_ref, which * slots, slots, 1, gathered, target)
 
     vmem = pl.BlockSpec(memory_space=pltpu.VMEM)
     smem = pl.BlockSpec(memory_space=pltpu.SMEM)
@@ -91,7 +91,7 @@
         compiler_params=pltpu.CompilerParams(vmem_limit_bytes=VMEM_BYTES),
         name="prepare",
     )(
-        planes, (ghosts * 4).reshape(1, -1), (parent_ghosts * 4).reshape(1, -1), operators
+        planes, (ghosts * 4).reshape(1, -1), parent_ghosts.reshape(1, -1), operators
     )
 
 
@@ -166,14 +166,16 @@
         pltpu.make_async_copy(lists_hbm.at[slot], chunk.at[slot], chunk_sem.at[slot]).start()
 
 
-def parent_level(own, came, lists, translations, inverse, block, group, chunk_steps):
+def parent_level(
+    own, came, lists, translations, inverse, to_child, block, group, chunk_steps
+):
     parents = own.shape[1]
     columns, _, slots, _ = came.shape
     count = parents + columns * slots
     first = RING * chunk_steps * group
 
     def kernel(
-        own_ref, came_ref, lists_hbm, operators_hbm, inverse_ref, out_ref,
+        own_ref, came_ref, lists_hbm, operators_hbm, inverse_ref, to_child_ref, out_ref,
         table, operators, total, result, chunk, chunk_sem, operator_sem,
     ):
         early, late = split_operator_copy(operators_hbm, operators, operator_sem, first)
@@ -196,16 +198,19 @@
         )
         check = total[...].reshape(4 * parents, 128).astype(jnp.bfloat16)
         result[...] = dot_nt(check, inverse_ref[...])
+        out_ref[pl.ds(3, 8 * parents, stride=4), :] = jnp.zeros((8 * parents, 128), jnp.float32)
         for k in range(3):
-            out_ref[k] = result[pl.ds(k, parents, stride=4), :].astype(jnp.bfloat16)
+            down = result[pl.ds(k, parents, stride=4), :].astype(jnp.bfloat16)
+            for c in range(8):
+                out_ref[pl.ds(4 * c + k, parents, stride=32), :] = dot_nt(down, to_child_ref[c])
 
     vmem = pl.BlockSpec(memory_space=pltpu.VMEM)
     hbm = pl.BlockSpec(memory_space=pl.ANY)
     return pl.pallas_call(
         kernel,
-        in_specs=[vmem, vmem, hbm, hbm, vmem],
+        in_specs=[vmem, vmem, hbm, hbm, vmem, vmem],
         out_specs=vmem,
-        out_shape=jax.ShapeDtypeStruct((3, parents, 128), jnp.bfloat16),
+        out_shape=jax.ShapeDtypeStruct((32 * parents, 128), jnp.float32),
         scratch_shapes=[
             pltpu.VMEM((4 * count + 16, 128), jnp.float32),
             pltpu.VMEM(translations.shape, translations.dtype),
@@ -217,51 +222,39 @@
         ],
         compiler_params=pltpu.CompilerParams(vmem_limit_bytes=VMEM_BYTES),
         name="parent_level",
-    )(own, came, lists, translations, inverse)
+    )(own, came, lists, translations, inverse, to_child)
 
 
 def leaf_level(
-    own, came, direct, origin, parent_down, lists, translations, to_child, inverse,
-    block, group, chunk_steps,
+    own, came, direct, origin, from_parent, lists, translations, inverse, block, group, chunk_steps,
 ):
     boxes = own.shape[1]
-    parents = boxes // 8
     offsets = origin.shape[1]
     slots = direct.shape[1]
     count = boxes + offsets * slots
     first = RING * chunk_steps * group // (boxes // block)
 
     def kernel(
-        origin_ref, own_ref, parent_ref, to_child_ref, inverse_ref, lists_hbm, operators_hbm,
-        came_hbm, direct_hbm, out_ref,
-        table, operators, ghosts, total, result, chunk, chunk_sem, operator_sem, ghost_sem,
+        origin_ref, own_ref, parent_hbm, inverse_ref, lists_hbm, operators_hbm, came_ref,
+        direct_ref, out_ref,
+        table, operators, total, result, chunk, chunk_sem, operator_sem, parent_sem,
     ):
-        def ghost_copy(source, j):
-            return pltpu.make_async_copy(source, ghosts.at[j], ghost_sem.at[j])
-
-        for j in range(offsets):
-            kind, place = origin_ref[0, j], origin_ref[1, j]
-            pl.when(kind == 0)(lambda: ghost_copy(came_hbm.at[place], j).start())
-            pl.when(kind == 1)(lambda: ghost_copy(direct_hbm, j).start())
         first_fetches(lists_hbm, chunk, chunk_sem)
         early, late = split_operator_copy(operators_hbm, operators, operator_sem, first)
         early.start()
+        parent_copy = pltpu.make_async_copy(parent_hbm, total, parent_sem)
+        parent_copy.start()
         late.start()
         table[0:8, :] = jnp.zeros((8, 128), jnp.float32)
         table[pl.ds(8 + 3, count, stride=4), :] = jnp.zeros((count, 128), jnp.float32)
         spread(table, 8, own_ref)
-        result[pl.ds(3, boxes, stride=4), :] = jnp.zeros((boxes, 128), jnp.float32)
-        for c in range(8):
-            for k in range(3):
-                result[pl.ds(4 * c + k, parents, stride=32), :] = dot_nt(
-                    parent_ref[k], to_child_ref[c]
-                )
-        for b in range(boxes // block):
-            total[b] = result[4 * block * b : 4 * block * (b + 1), :]
         for j in range(offsets):
-            ghost_copy(direct_hbm, j).wait()
-            spread(table, 8 + 4 * (boxes + j * slots), ghosts.at[j])
+            at = 8 + 4 * (boxes + j * slots)
+            spread(table, at, came_ref.at[origin_ref[1, j]])
+            if j % NEAR == NEAR - 1:
+                pl.when(origin_ref[0, j] == 1)(lambda: spread(table, at, direct_ref))
         early.wait()
+        parent_copy.wait()
 
         def at_turn(turn):
             pl.when(turn == 1)(lambda: late.wait())
@@ -282,24 +275,30 @@
     hbm = pl.BlockSpec(memory_space=pl.ANY)
     return pl.pallas_call(
         kernel,
-        in_specs=[smem, vmem, vmem, vmem, vmem, hbm, hbm, hbm, hbm],
+        in_specs=[smem, vmem, hbm, vmem, hbm, hbm, vmem, vmem],
         out_specs=vmem,
         out_shape=jax.ShapeDtypeStruct((3, boxes, 128), jnp.bfloat16),
         scratch_shapes=[
             pltpu.VMEM((4 * count + 16, 128), jnp.float32),
             pltpu.VMEM(translations.shape, translations.dtype),
-            pltpu.VMEM((offsets, 3, slots, 128), jnp.bfloat16),
             pltpu.VMEM((boxes // block, 4 * block, 128), jnp.float32),
             pltpu.VMEM((4 * boxes, 128), jnp.float32),
             pltpu.SMEM((RING, 1, chunk_steps * block * group), jnp.int32),
             pltpu.SemaphoreType.DMA((RING,)),
             pltpu.SemaphoreType.DMA((2,)),
-            pltpu.SemaphoreType.DMA((offsets,)),
+            pltpu.SemaphoreType.DMA,
         ],
         compiler_params=pltpu.CompilerParams(vmem_limit_bytes=VMEM_BYTES),
         name="leaf_level",
     )(
-        origin, own, parent_down, to_child, inverse, lists, translations, came, direct
+        origin,
+        own,
+        from_parent.reshape(boxes // block, 4 * block, 128),
+        inverse,
+        lists,
+        translations,
+        came,
+        direct,
     )
 
 
@@ -355,29 +354,29 @@
     kept = lax.dynamic_slice_in_dim(sent, start, NEAR - 1)
     shifted = jnp.where(foreign[:, None, None, None], shifted, kept)
     sent = lax.dynamic_update_slice_in_dim(sent, shifted, start, 0)
-    sent, direct, parent_came = lax.optimization_barrier((sent, direct, parent_came))
+    sent, parent_came = lax.optimization_barrier((sent, parent_came))
     came = lax.all_to_all(sent, "col", split_axis=0, concat_axis=0, tiled=True)
-    parent_down = parent_level(
+    from_parent = parent_level(
         parent_up,
         parent_came,
         order_lists(parent_lists, 64, 4, 8),
         translations,
         check_to_density,
+        parent_to_child,
         64,
         4,
         8,
     )
     lists = order_lists(leaf_lists, 256, 4, 4)
-    came, parent_down, lists = lax.optimization_barrier((came, parent_down, lists))
+    came, from_parent, lists = lax.optimization_barrier((came, from_parent, lists))
     leaf_down = leaf_level(
         planes,
         came,
         direct,
         message_origin(column, columns),
-        parent_down,
+        from_parent,
         lists,
         translations,
-        parent_to_child,
         check_to_density,
         256,
         4,

time: 190 us -> 190 us (level)
  waiting for transfers between devices: 22.7 us -> 17.2 us
  starting transfers between devices: 20.2 us -> 25 us
    all_to_all x1, waiting for transfers between devices: 15.9 us -> 8.48 us  [local(): came = lax.all_to_all(sent, 'col', split_axis=0, concat_axis=0, tiled=True)]
    all_to_all x1, starting transfers between devices: 5.4 us -> 8.88 us  [local(): lax.all_to_all(parent_sent, 'col', split_axis=0, concat_axis=0, tiled=True)]
    ppermute x1, waiting for transfers between devices: 6.75 us -> 8.68 us  [local(): lax.ppermute(passing, ('row', 'col'), [p for p in turn if p[1] in ranks])]
    unnamed x11 -> x9, local copies, waits for them, and re-layouts: 3.87 us -> 3.83 us
  transfers between devices with their start and end apart: 4 -> 4, of which waited for: 2 -> 2; matrix products, arithmetic and copies ran while one was open for 8% -> 8% of each run, Pallas kernels for 9% -> 10%
where the time goes in v4:
time: 190 us; the launch traced here: 187 us
  Pallas kernels  124 us (65%)
  starting transfers between devices  25 us (13%)
  waiting for transfers between devices  17.2 us (9%)
  local copies, waits for them, and re-layouts  14 us (7%)
  other arithmetic  6.51 us (3%)
    pallas_call x1, Pallas kernels, leaf_level(): pl.pallas_call(kernel, in_specs=[smem, vmem, hbm, vmem, hbm, hbm, vmem, v...  97.6 us
    pallas_call x1, Pallas kernels, parent_level(): pl.pallas_call(kernel, in_specs=[vmem, vmem, hbm, hbm, vmem, vmem], out_s...  18.3 us
    all_to_all x1, starting transfers between devices, local(): lax.all_to_all(parent_sent, 'col', split_axis=0, concat_axis=0, tiled=True)  8.88 us
    ppermute x1, waiting for transfers between devices, local(): lax.ppermute(passing, ('row', 'col'), [p for p in turn if p[1] in ranks])  8.68 us
    all_to_all x1, waiting for transfers between devices, local(): came = lax.all_to_all(sent, 'col', split_axis=0, concat_axis=0, tiled=True)  8.48 us
    pallas_call x1, Pallas kernels, prepare(): pl.pallas_call(kernel, in_specs=[vmem, smem, smem, vmem], out_specs=[vmem...  8.26 us
    all_to_all x1, starting transfers between devices, local(): came = lax.all_to_all(sent, 'col', split_axis=0, concat_axis=0, tiled=True)  6.83 us
    ppermute x1, starting transfers between devices, local(): lax.ppermute(direct, ('row', 'col'), [p for p in half if p[1] in ranks])  6.67 us
  transfers between devices with their start and end apart: 4, of which 2 were waited for; matrix products, arithmetic and copies ran while one was open for 8% of the time, Pallas kernels for 10%

profile of v4, /device:TPU:3, one launch (start us, length us, event | category | flops | bytes accessed | tf_op | source)
XLA Modules:
  0.0 187.1 jit_solution(7034819458662867130)
XLA Ops:
  0.0 0.0 copy-start
  0.0 0.1 fusion.3
  0.1 0.6 copy-done
  0.7 0.6 gather_fusion
  1.3 0.6 copy.13
  2.0 1.4 reshape_squeeze.3.parent_ghosts_ref
  3.3 8.3 %prepare.1 = (bf16[16,3,256,128]{3,2,1,0:T(8,128)(2,1)}, bf16[7,3,256,128]{3,2,1,0:T(8,128)(2,1)}, bf16[3,256,128]{2,1,0:T(8,128)(2,1)}, bf16[3,64,128]{2,1,0:T(8,128)(2,1)}, bf16[16,3,32,128]{3,2,1,0:T(8,128)(2,1)}) custom-call(bf16[3,512,128]{2,1,0:T(8,128)(2,1)} %bitcast.30, s32[1,6144]{1,0:T(1,128)} %bitcast.32, ...), custom_call_target="tpu_custom_call" | custom-call | tf_op jit(solution)/shard_map/prepare/pallas_call | solution.py:74
  11.6 2.6 %collective-permute-start = (bf16[7,3,256,128]{3,2,1,0:T(8,128)(2,1)}, bf16[7,3,256,128]{3,2,1,0:T(8,128)(2,1)S(1)}, u32[]{:S(2)}, u32[]{:S(2)}) collective-permute-start(bf16[7,3,256,128]{3,2,1,0:T(8,128)(2,1)} %get-tuple-element.16), channel_id=1, source_target_pairs={{8,24},{9,25},{10,26},{11,27},{12,28},{13,29},{14,30},{15,31},{16,... | collective-permute-start | bytes 4128776 | tf_op jit(solution)/shard_map/ppermute | solution.py:350
  14.2 8.9 %all-to-all-start = ((bf16[16,3,32,128]{3,2,1,0:T(8,128)(2,1)}), bf16[16,3,32,128]{3,2,1,0:T(8,128)(2,1)S(1)}, u32[]{:S(2)}, u32[]{:S(2)}) async-start(bf16[16,3,32,128]{3,2,1,0:T(8,128)(2,1)} %get-tuple-element.17), calls=%async_computation | async-start | bytes 786432 | tf_op jit(solution)/shard_map/all_to_all | solution.py:347
  23.1 8.7 %collective-permute-done = bf16[7,3,256,128]{3,2,1,0:T(8,128)(2,1)S(1)} collective-permute-done((bf16[7,3,256,128]{3,2,1,0:T(8,128)(2,1)}, bf16[7,3,256,128]{3,2,1,0:T(8,128)(2,1)S(1)}, u32[]{:S(2)}, u32[]{:S(2)}) %collective-permute-start) | collective-permute-done | bytes 1376288 | tf_op jit(solution)/shard_map/ppermute | solution.py:350
  31.8 2.9 %select_dynamic-update-slice_fusion = bf16[16,3,256,128]{3,2,1,0:T(8,128)(2,1)} fusion(bf16[16,3,256,128]{3,2,1,0:T(8,128)(2,1)} %get-tuple-element.15, s32[]{:T(128)S(6)} %select_n.174, bf16[7,3,256,128]{3,2,1,0:T(8,128)(2,1)S(1)} %collective-permute-done, pred[7]{0:T(512)(128)(4,1)S(1)} %abs_compare_fusion), kind=kLoop, calls=%fused_computation.1 | loop fusion | flops 688128 | bytes 4128779 | tf_op jit(solution)/shard_map/dynamic_update_slice | solution.py:356
  34.7 0.0 all-to-all-done.came_ref
  34.7 0.0 copy-start.2
  34.7 0.7 copy-done.2
  35.4 6.8 %all-to-all-start.1 = ((bf16[16,3,256,128]{3,2,1,0:T(8,128)(2,1)}), bf16[16,3,256,128]{3,2,1,0:T(8,128)(2,1)S(1)}, u32[]{:S(2)}, u32[]{:S(2)}) async-start(bf16[16,3,256,128]{3,2,1,0:T(8,128)(2,1)} %select_dynamic-update-slice_fusion), calls=%async_computation.1 | async-start | bytes 6291456 | tf_op jit(solution)/shard_map/all_to_all | solution.py:358
  42.2 6.7 %collective-permute-start.1 = (bf16[3,256,128]{2,1,0:T(8,128)(2,1)}, bf16[3,256,128]{2,1,0:T(8,128)(2,1)}, u32[]{:S(2)}, u32[]{:S(2)}) collective-permute-start(bf16[3,256,128]{2,1,0:T(8,128)(2,1)} %get-tuple-element.24), channel_id=1, source_target_pairs={{8,16},{9,17},{10,18},{11,19},{12,20},{13,21},{14,22},{15,23},{16,... | collective-permute-start | bytes 589832 | tf_op jit(solution)/shard_map/ppermute | solution.py:352
  48.9 0.9 multiply_bitcast_fusion.1
  49.8 0.1 copy.11
  49.9 0.1 reshape_transpose_reshape.3
  50.1 0.7 reshape.206.lists_hbm
  50.8 2.0 %multiply_bitcast_fusion = s32[316,512]{1,0:T(8,128)} fusion(s32[512,316]{0,1:T(8,128)} %param.14), kind=kLoop, calls=%fused_computation.2 | loop fusion | flops 323584 | bytes 1294336 | tf_op jit(solution)/shard_map/transpose | solution.py:101
  52.8 2.3 %reshape.207 = s32[79,4,2,256]{3,2,1,0:T(2,128)} reshape(s32[316,512]{1,0:T(8,128)} %multiply_bitcast_fusion) | data formatting | bytes 1294336 | tf_op jit(solution)/shard_map/reshape | solution.py:101
  55.1 1.3 copy.12
  56.4 0.1 pad.8
  56.5 0.1 copy.14
  56.6 0.9 concatenate.39
  57.5 2.8 %reshape.209.lists_hbm = s32[42,1,4096]{2,1,0:T(1,128)} reshape(s32[168,1024]{1,0:T(8,128)} %concatenate.39) | data formatting | bytes 1376256 | tf_op jit(solution)/shard_map/reshape | solution.py:107
  60.3 0.6 pad_add_fusion.origin_ref
  60.9 18.3 %parent_level.1 = f32[2048,128]{1,0:T(8,128)} custom-call(bf16[3,64,128]{2,1,0:T(8,128)(2,1)} %get-tuple-element.19.own_ref, bf16[16,3,32,128]{3,2,1,0:T(8,128)(2,1)} %copy-done.2, s32[12,1,2048]{2,1,0:T(1,128)} %reshape.206.lists_hbm, bf16[316,128,128]{2,1,0:T(8,128)(2,1)} %operators_hbm.3, bf16[128,128]{1,0:T(8,128)(2,1)} %inverse_ref.3, ...), custom_call_target="tpu_custom_call" | custom-call | tf_op jit(solution)/shard_map/parent_level/pallas_call | solution.py:209
  79.2 8.5 %all-to-all-done.1.came_ref = bf16[16,3,256,128]{3,2,1,0:T(8,128)(2,1)S(1)} async-done(((bf16[16,3,256,128]{3,2,1,0:T(8,128)(2,1)}), bf16[16,3,256,128]{3,2,1,0:T(8,128)(2,1)S(1)}, u32[]{:S(2)}, u32[]{:S(2)}) %all-to-all-start.1) | async-done | bytes 3145760 | tf_op jit(solution)/shard_map/all_to_all | solution.py:358
  87.6 0.0 copy-start.1
  87.6 0.0 collective-permute-done.1.direct_ref
  87.6 1.6 copy-done.1
  89.3 97.6 %leaf_level.1 = bf16[3,512,128]{2,1,0:T(8,128)(2,1)} custom-call(s32[2,16]{1,0:T(2,128)} %pad_add_fusion.origin_ref, bf16[3,512,128]{2,1,0:T(8,128)(2,1)} %bitcast.31, f32[2,1024,128]{2,1,0:T(8,128)} %bitcast.25, bf16[128,128]{1,0:T(8,128)(2,1)} %inverse_ref.3, s32[42,1,4096]{2,1,0:T(1,128)} %reshape.209.lists_hbm, bf16[316,128,128]{2,1,0:T(8,128)(2,1)} %operators_hbm.3, ...), custom_call_target="tpu_custom_call" | custom-call | tf_op jit(solution)/shard_map/leaf_level/pallas_call | solution.py:276
  (7 shorter events, 0.1 us)
Async XLA Ops:
  0.0 0.7 copy-start
  11.6 20.2 %collective-permute-start = (bf16[7,3,256,128]{3,2,1,0:T(8,128)(2,1)}, bf16[7,3,256,128]{3,2,1,0:T(8,128)(2,1)S(1)}, u32[]{:S(2)}, u32[]{:S(2)}) collective-permute-start(bf16[7,3,256,128]{3,2,1,0:T(8,128)(2,1)} %get-tuple-element.16), channel_id=1, source_target_pairs={{8,24},{9,25},{10,26},{11,27},{12,28},{13,29},{14,30},{15,31},{16,... | collective-permute-start | bytes 4128776 | tf_op jit(solution)/shard_map/ppermute | solution.py:350
  14.2 20.5 %all-to-all-start = ((bf16[16,3,32,128]{3,2,1,0:T(8,128)(2,1)}), bf16[16,3,32,128]{3,2,1,0:T(8,128)(2,1)S(1)}, u32[]{:S(2)}, u32[]{:S(2)}) async-start(bf16[16,3,32,128]{3,2,1,0:T(8,128)(2,1)} %get-tuple-element.17), calls=%async_computation | async-start | bytes 786432 | tf_op jit(solution)/shard_map/all_to_all | solution.py:347
  34.7 0.7 copy-start.2
  35.4 52.2 %all-to-all-start.1 = ((bf16[16,3,256,128]{3,2,1,0:T(8,128)(2,1)}), bf16[16,3,256,128]{3,2,1,0:T(8,128)(2,1)S(1)}, u32[]{:S(2)}, u32[]{:S(2)}) async-start(bf16[16,3,256,128]{3,2,1,0:T(8,128)(2,1)} %select_dynamic-update-slice_fusion), calls=%async_computation.1 | async-start | bytes 6291456 | tf_op jit(solution)/shard_map/all_to_all | solution.py:358
  42.2 45.4 %collective-permute-start.1 = (bf16[3,256,128]{2,1,0:T(8,128)(2,1)}, bf16[3,256,128]{2,1,0:T(8,128)(2,1)}, u32[]{:S(2)}, u32[]{:S(2)}) collective-permute-start(bf16[3,256,128]{2,1,0:T(8,128)(2,1)} %get-tuple-element.24), channel_id=1, source_target_pairs={{8,16},{9,17},{10,18},{11,19},{12,20},{13,21},{14,22},{15,23},{16,... | collective-permute-start | bytes 589832 | tf_op jit(solution)/shard_map/ppermute | solution.py:352
  87.6 1.6 copy-start.1

commit v5 on v4

--- a/solution.py
+++ b/solution.py
@@ -354,7 +354,7 @@
     kept = lax.dynamic_slice_in_dim(sent, start, NEAR - 1)
     shifted = jnp.where(foreign[:, None, None, None], shifted, kept)
     sent = lax.dynamic_update_slice_in_dim(sent, shifted, start, 0)
-    sent, parent_came = lax.optimization_barrier((sent, parent_came))
+    sent, direct, parent_came = lax.optimization_barrier((sent, direct, parent_came))
     came = lax.all_to_all(sent, "col", split_axis=0, concat_axis=0, tiled=True)
     from_parent = parent_level(
         parent_up,

time: 190 us -> 190 us (level)
  starting transfers between devices: 25 us -> 20.2 us
  waiting for transfers between devices: 17.2 us -> 21.4 us
    all_to_all x1, waiting for transfers between devices: 8.48 us -> 14.6 us  [local(): came = lax.all_to_all(sent, 'col', split_axis=0, concat_axis=0, tiled=True)]
    all_to_all x1, starting transfers between devices: 8.88 us -> 5.4 us  [local(): lax.all_to_all(parent_sent, 'col', split_axis=0, concat_axis=0, tiled=True)]
    ppermute x1, waiting for transfers between devices: 8.68 us -> 6.75 us  [local(): lax.ppermute(passing, ('row', 'col'), [p for p in turn if p[1] in ranks])]
    unnamed x9 -> x11, local copies, waits for them, and re-layouts: 3.83 us -> 3.87 us
where the time goes in v5:
time: 190 us; the launch traced here: 187 us
  Pallas kernels  124 us (65%)
  waiting for transfers between devices  21.4 us (11%)
  starting transfers between devices  20.2 us (11%)
  local copies, waits for them, and re-layouts  14 us (7%)
  other arithmetic  6.51 us (3%)
    pallas_call x1, Pallas kernels, leaf_level(): pl.pallas_call(kernel, in_specs=[smem, vmem, hbm, vmem, hbm, hbm, vmem, v...  97.6 us
    pallas_call x1, Pallas kernels, parent_level(): pl.pallas_call(kernel, in_specs=[vmem, vmem, hbm, hbm, vmem, vmem], out_s...  18.3 us
    all_to_all x1, waiting for transfers between devices, local(): came = lax.all_to_all(sent, 'col', split_axis=0, concat_axis=0, tiled=True)  14.6 us
    pallas_call x1, Pallas kernels, prepare(): pl.pallas_call(kernel, in_specs=[vmem, smem, smem, vmem], out_specs=[vmem...  8.25 us
    all_to_all x1, starting transfers between devices, local(): came = lax.all_to_all(sent, 'col', split_axis=0, concat_axis=0, tiled=True)  6.84 us
    ppermute x1, waiting for transfers between devices, local(): lax.ppermute(passing, ('row', 'col'), [p for p in turn if p[1] in ranks])  6.75 us
    ppermute x1, starting transfers between devices, local(): lax.ppermute(direct, ('row', 'col'), [p for p in half if p[1] in ranks])  5.4 us
    all_to_all x1, starting transfers between devices, local(): lax.all_to_all(parent_sent, 'col', split_axis=0, concat_axis=0, tiled=True)  5.4 us
  transfers between devices with their start and end apart: 4, of which 2 were waited for; matrix products, arithmetic and copies ran while one was open for 8% of the time, Pallas kernels for 10%

profile of v5, /device:TPU:3, one launch (start us, length us, event | category | flops | bytes accessed | tf_op | source)
XLA Modules:
  0.0 186.5 jit_solution(12164034794196285593)
XLA Ops:
  0.0 0.0 copy-start
  0.0 0.1 fusion.3
  0.1 0.6 copy-done
  0.7 0.6 gather_fusion
  1.3 0.6 copy.13
  1.9 1.3 reshape_squeeze.3.parent_ghosts_ref
  3.3 8.2 %prepare.1 = (bf16[16,3,256,128]{3,2,1,0:T(8,128)(2,1)}, bf16[7,3,256,128]{3,2,1,0:T(8,128)(2,1)}, bf16[3,256,128]{2,1,0:T(8,128)(2,1)}, bf16[3,64,128]{2,1,0:T(8,128)(2,1)}, bf16[16,3,32,128]{3,2,1,0:T(8,128)(2,1)}) custom-call(bf16[3,512,128]{2,1,0:T(8,128)(2,1)} %bitcast.30, s32[1,6144]{1,0:T(1,128)} %bitcast.32, ...), custom_call_target="tpu_custom_call" | custom-call | tf_op jit(solution)/shard_map/prepare/pallas_call | solution.py:74
  11.5 2.6 %collective-permute-start = (bf16[7,3,256,128]{3,2,1,0:T(8,128)(2,1)}, bf16[7,3,256,128]{3,2,1,0:T(8,128)(2,1)S(1)}, u32[]{:S(2)}, u32[]{:S(2)}) collective-permute-start(bf16[7,3,256,128]{3,2,1,0:T(8,128)(2,1)} %get-tuple-element.17), channel_id=1, source_target_pairs={{8,24},{9,25},{10,26},{11,27},{12,28},{13,29},{14,30},{15,31},{16,... | collective-permute-start | bytes 4128776 | tf_op jit(solution)/shard_map/ppermute | solution.py:350
  14.1 5.4 %collective-permute-start.1 = (bf16[3,256,128]{2,1,0:T(8,128)(2,1)}, bf16[3,256,128]{2,1,0:T(8,128)(2,1)S(1)}, u32[]{:S(2)}, u32[]{:S(2)}) collective-permute-start(bf16[3,256,128]{2,1,0:T(8,128)(2,1)} %get-tuple-element.18), channel_id=1, source_target_pairs={{8,16},{9,17},{10,18},{11,19},{12,20},{13,21},{14,22},{15,23},{16,... | collective-permute-start | bytes 589832 | tf_op jit(solution)/shard_map/ppermute | solution.py:352
  19.5 5.4 %all-to-all-start = ((bf16[16,3,32,128]{3,2,1,0:T(8,128)(2,1)}), bf16[16,3,32,128]{3,2,1,0:T(8,128)(2,1)S(1)}, u32[]{:S(2)}, u32[]{:S(2)}) async-start(bf16[16,3,32,128]{3,2,1,0:T(8,128)(2,1)} %get-tuple-element.19), calls=%async_computation | async-start | bytes 786432 | tf_op jit(solution)/shard_map/all_to_all | solution.py:347
  24.9 6.8 %collective-permute-done = bf16[7,3,256,128]{3,2,1,0:T(8,128)(2,1)S(1)} collective-permute-done((bf16[7,3,256,128]{3,2,1,0:T(8,128)(2,1)}, bf16[7,3,256,128]{3,2,1,0:T(8,128)(2,1)S(1)}, u32[]{:S(2)}, u32[]{:S(2)}) %collective-permute-start) | collective-permute-done | bytes 1376288 | tf_op jit(solution)/shard_map/ppermute | solution.py:350
  31.7 2.9 %select_dynamic-update-slice_fusion = bf16[16,3,256,128]{3,2,1,0:T(8,128)(2,1)} fusion(bf16[16,3,256,128]{3,2,1,0:T(8,128)(2,1)} %get-tuple-element.16, s32[]{:T(128)S(6)} %select_n.174, bf16[7,3,256,128]{3,2,1,0:T(8,128)(2,1)S(1)} %collective-permute-done, pred[7]{0:T(512)(128)(4,1)S(1)} %abs_compare_fusion), kind=kLoop, calls=%fused_computation.1 | loop fusion | flops 688128 | bytes 4128779 | tf_op jit(solution)/shard_map/dynamic_update_slice | solution.py:356
  34.6 0.0 collective-permute-done.1.direct_ref
  34.6 0.0 copy-start.3
  34.6 0.0 all-to-all-done.came_ref
  34.6 0.0 copy-start.2
  34.6 0.7 copy-done.3
  35.3 0.1 copy-done.2
  35.4 6.8 %all-to-all-start.1 = ((bf16[16,3,256,128]{3,2,1,0:T(8,128)(2,1)}), bf16[16,3,256,128]{3,2,1,0:T(8,128)(2,1)S(1)}, u32[]{:S(2)}, u32[]{:S(2)}) async-start(bf16[16,3,256,128]{3,2,1,0:T(8,128)(2,1)} %select_dynamic-update-slice_fusion), calls=%async_computation.1 | async-start | bytes 6291456 | tf_op jit(solution)/shard_map/all_to_all | solution.py:358
  42.2 0.9 multiply_bitcast_fusion.1
  43.1 0.1 copy.11
  43.3 0.1 reshape_transpose_reshape.3
  43.4 0.7 reshape.206.lists_hbm
  44.1 2.0 %multiply_bitcast_fusion = s32[316,512]{1,0:T(8,128)} fusion(s32[512,316]{0,1:T(8,128)} %param.14), kind=kLoop, calls=%fused_computation.2 | loop fusion | flops 323584 | bytes 1294336 | tf_op jit(solution)/shard_map/transpose | solution.py:101
  46.1 2.3 %reshape.207 = s32[79,4,2,256]{3,2,1,0:T(2,128)} reshape(s32[316,512]{1,0:T(8,128)} %multiply_bitcast_fusion) | data formatting | bytes 1294336 | tf_op jit(solution)/shard_map/reshape | solution.py:101
  48.4 1.3 copy.12
  49.7 0.1 pad.8
  49.8 0.1 copy.14
  49.9 0.9 concatenate.39
  50.8 2.8 %reshape.209.lists_hbm = s32[42,1,4096]{2,1,0:T(1,128)} reshape(s32[168,1024]{1,0:T(8,128)} %concatenate.39) | data formatting | bytes 1376256 | tf_op jit(solution)/shard_map/reshape | solution.py:107
  53.6 0.6 pad_add_fusion.origin_ref
  54.2 18.3 %parent_level.1 = f32[2048,128]{1,0:T(8,128)} custom-call(bf16[3,64,128]{2,1,0:T(8,128)(2,1)} %get-tuple-element.21.own_ref, bf16[16,3,32,128]{3,2,1,0:T(8,128)(2,1)} %copy-done.2, s32[12,1,2048]{2,1,0:T(1,128)} %reshape.206.lists_hbm, bf16[316,128,128]{2,1,0:T(8,128)(2,1)} %operators_hbm.3, bf16[128,128]{1,0:T(8,128)(2,1)} %inverse_ref.3, ...), custom_call_target="tpu_custom_call" | custom-call | tf_op jit(solution)/shard_map/parent_level/pallas_call | solution.py:209
  72.5 14.6 %all-to-all-done.1.came_ref = bf16[16,3,256,128]{3,2,1,0:T(8,128)(2,1)S(1)} async-done(((bf16[16,3,256,128]{3,2,1,0:T(8,128)(2,1)}), bf16[16,3,256,128]{3,2,1,0:T(8,128)(2,1)S(1)}, u32[]{:S(2)}, u32[]{:S(2)}) %all-to-all-start.1) | async-done | bytes 3145760 | tf_op jit(solution)/shard_map/all_to_all | solution.py:358
  87.1 0.0 copy-start.1
  87.1 1.6 copy-done.1
  88.8 97.6 %leaf_level.1 = bf16[3,512,128]{2,1,0:T(8,128)(2,1)} custom-call(s32[2,16]{1,0:T(2,128)} %pad_add_fusion.origin_ref, bf16[3,512,128]{2,1,0:T(8,128)(2,1)} %bitcast.31, f32[2,1024,128]{2,1,0:T(8,128)} %bitcast.25, bf16[128,128]{1,0:T(8,128)(2,1)} %inverse_ref.3, s32[42,1,4096]{2,1,0:T(1,128)} %reshape.209.lists_hbm, bf16[316,128,128]{2,1,0:T(8,128)(2,1)} %operators_hbm.3, ...), custom_call_target="tpu_custom_call" | custom-call | tf_op jit(solution)/shard_map/leaf_level/pallas_call | solution.py:276
  (7 shorter events, 0.1 us)
Async XLA Ops:
  0.0 0.7 copy-start
  11.5 20.2 %collective-permute-start = (bf16[7,3,256,128]{3,2,1,0:T(8,128)(2,1)}, bf16[7,3,256,128]{3,2,1,0:T(8,128)(2,1)S(1)}, u32[]{:S(2)}, u32[]{:S(2)}) collective-permute-start(bf16[7,3,256,128]{3,2,1,0:T(8,128)(2,1)} %get-tuple-element.17), channel_id=1, source_target_pairs={{8,24},{9,25},{10,26},{11,27},{12,28},{13,29},{14,30},{15,31},{16,... | collective-permute-start | bytes 4128776 | tf_op jit(solution)/shard_map/ppermute | solution.py:350
  14.1 20.5 %collective-permute-start.1 = (bf16[3,256,128]{2,1,0:T(8,128)(2,1)}, bf16[3,256,128]{2,1,0:T(8,128)(2,1)S(1)}, u32[]{:S(2)}, u32[]{:S(2)}) collective-permute-start(bf16[3,256,128]{2,1,0:T(8,128)(2,1)} %get-tuple-element.18), channel_id=1, source_target_pairs={{8,16},{9,17},{10,18},{11,19},{12,20},{13,21},{14,22},{15,23},{16,... | collective-permute-start | bytes 589832 | tf_op jit(solution)/shard_map/ppermute | solution.py:352
  19.5 15.1 %all-to-all-start = ((bf16[16,3,32,128]{3,2,1,0:T(8,128)(2,1)}), bf16[16,3,32,128]{3,2,1,0:T(8,128)(2,1)S(1)}, u32[]{:S(2)}, u32[]{:S(2)}) async-start(bf16[16,3,32,128]{3,2,1,0:T(8,128)(2,1)} %get-tuple-element.19), calls=%async_computation | async-start | bytes 786432 | tf_op jit(solution)/shard_map/all_to_all | solution.py:347
  34.6 0.7 copy-start.3
  34.6 0.8 copy-start.2
  35.4 51.7 %all-to-all-start.1 = ((bf16[16,3,256,128]{3,2,1,0:T(8,128)(2,1)}), bf16[16,3,256,128]{3,2,1,0:T(8,128)(2,1)S(1)}, u32[]{:S(2)}, u32[]{:S(2)}) async-start(bf16[16,3,256,128]{3,2,1,0:T(8,128)(2,1)} %select_dynamic-update-slice_fusion), calls=%async_computation.1 | async-start | bytes 6291456 | tf_op jit(solution)/shard_map/all_to_all | solution.py:358
  87.1 1.6 copy-start.1
